TPU v7x, 512 devices: a whole 4x4x16 slice. The times are simulated.
512 devices in a mesh: dp: 16 (over y, x_hi, core), layer: 16 (over z), rep: 2 (over x_lo).
Axes of the slice: x: 4 (x_hi: 2, x_lo: 2; x = x_hi * 2 + x_lo), y: 4, z: 16, core: 2. Of those that a mesh axis runs over, the one named last changes fastest.
Arguments:
- grads: bfloat16 [4096, 40960], P('dp', 'layer'), may hold values from -4000 to 4000
Outputs:
- cosine: float32 [4096, 4096], P('dp', ('layer', 'rep'))
All inputs are finite; a program needn't handle non-finite values.
Results may differ from a plain program's by a relative error of at most 0.0003.
Values may be sent and summed in bfloat16 or wider, within the bound.
A program may use at most 64 MiB of HBM per device.

v0:
```python
import jax
import jax.numpy as jnp
from jax import lax
from jax.sharding import PartitionSpec as P


def from_behind(array, axis, by):
    length = lax.axis_size(axis)
    return lax.ppermute(array, axis, [(i, (i + by) % length) for i in range(length)])


def body(grads):
    row_count = grads.shape[0]
    cycle_size = lax.axis_size("dp")
    half_cycle = cycle_size // 2
    step_count = half_cycle // 2 + 1
    dp_index = lax.axis_index("dp")
    rep_index = lax.axis_index("rep")
    examples = row_count * cycle_size
    squares = jnp.sum(jnp.square(grads.astype(jnp.float32)), axis=1)
    group_total = lax.psum(squares, "layer")
    norm_values = lax.all_gather(group_total, "dp", axis=0, tiled=True)
    inverse = lax.rsqrt(norm_values + 1e-06)
    far_grads = from_behind(grads, "dp", -half_cycle)
    first_offset = rep_index * half_cycle
    stride = 1
    visiting = jnp.where(rep_index == 0, grads, far_grads)
    products = []
    flips = []
    columns = []
    for turn in range(step_count):
        if turn > 0:
            visiting = from_behind(visiting, "dp", -1)
        offset = first_offset + stride * turn
        usable = jnp.logical_or(turn < step_count - 1, rep_index == 0)
        usable = jnp.logical_and(
            usable, jnp.logical_or(offset != half_cycle, dp_index < half_cycle)
        )
        product = lax.dot_general(
            grads, visiting, (((1,), (1,)), ((), ())), preferred_element_type=jnp.float32
        )
        product = jnp.where(usable, product, 0.0)
        sends = jnp.logical_and(usable, offset != 0)
        products.append(product)
        flips.append(jnp.where(sends, product.T, 0.0))
        columns.append((dp_index + offset) % cycle_size)
    zero_index = jnp.int32(0)
    own_tiles = jnp.zeros((row_count, cycle_size, row_count), jnp.float32)
    mirror_tiles = jnp.zeros((row_count, cycle_size, row_count), jnp.float32)
    for turn in range(step_count):
        own_tiles = lax.dynamic_update_slice(
            own_tiles, products[turn][:, None, :], (zero_index, columns[turn], zero_index)
        )
        mirror_tiles = lax.dynamic_update_slice(
            mirror_tiles, flips[turn][:, None, :], (zero_index, columns[turn], zero_index)
        )
    received = lax.all_to_all(mirror_tiles, "dp", split_axis=1, concat_axis=1, tiled=True)
    combined = (own_tiles + received).reshape(row_count, examples)
    reduced = lax.psum_scatter(combined, ("layer", "rep"), scatter_dimension=1, tiled=True)
    width = reduced.shape[1]
    span_index = lax.axis_index(("layer", "rep"))
    column_inverse = lax.dynamic_slice_in_dim(inverse, span_index * width, width)
    row_inverse = lax.dynamic_slice_in_dim(inverse, dp_index * row_count, row_count)
    return reduced * row_inverse[:, None] * column_inverse[None, :]


def solution(mesh):
    in_specs = (P("dp", "layer"),)
    out_specs = P("dp", ("layer", "rep"))
    return jax.shard_map(body, mesh=mesh, in_specs=in_specs, out_specs=out_specs, check_vma=False)
```

profile of v0, /device:TPU:24, one launch (start us, length us, event | category | flops | bytes accessed | tf_op | source)
XLA Modules:
  0.0 363.4 jit_solution(10651847105386602982)
XLA Ops:
  6.5 0.0 reduce-scatter.2.cloned.1.call-start
  6.5 3.1 collective-permute-start
  9.7 31.0 %collective-permute-done = bf16[256,2560]{1,0:T(8,128)(2,1)S(1)} collective-permute-done((bf16[256,2560]{1,0:T(8,128)(2,1)}, bf16[256,2560]{1,0:T(8,128)(2,1)S(1)}, u32[]{:S(2)}, u32[]{:S(2)}) %collective-permute-start) | collective-permute-done | bytes 1310752 | tf_op jit(solution)/shard_map/ppermute | solution.py:9
  40.7 1.5 broadcast_select_fusion
  42.1 3.7 %collective-permute-start.1 = (bf16[256,2560]{1,0:T(8,128)(2,1)S(1)}, bf16[256,2560]{1,0:T(8,128)(2,1)}, u32[]{:S(2)}, u32[]{:S(2)}) collective-permute-start(bf16[256,2560]{1,0:T(8,128)(2,1)S(1)} %broadcast_select_fusion), channel_id=1, source_target_pairs={{0,480},{32,0},{64,32},{96,64},{128,96},{160,128},{192,160},{224,1... | collective-permute-start | bytes 3932168 | tf_op jit(solution)/shard_map/ppermute | solution.py:9
  45.8 15.1 %collective-permute-done.1 = bf16[256,2560]{1,0:T(8,128)(2,1)} collective-permute-done((bf16[256,2560]{1,0:T(8,128)(2,1)S(1)}, bf16[256,2560]{1,0:T(8,128)(2,1)}, u32[]{:S(2)}, u32[]{:S(2)}) %collective-permute-start.1) | collective-permute-done | bytes 1310752 | tf_op jit(solution)/shard_map/ppermute | solution.py:9
  60.9 6.3 %collective-permute-start.2 = (bf16[256,2560]{1,0:T(8,128)(2,1)}, bf16[256,2560]{1,0:T(8,128)(2,1)}, u32[]{:S(2)}, u32[]{:S(2)}) collective-permute-start(bf16[256,2560]{1,0:T(8,128)(2,1)} %collective-permute-done.1), channel_id=1, source_target_pairs={{0,480},{32,0},{64,32},{96,64},{128,96},{160,128},{192,160},{224,1... | collective-permute-start | bytes 3932168 | tf_op jit(solution)/shard_map/ppermute | solution.py:9
  67.3 0.0 copy-start
  67.4 15.3 %collective-permute-done.2 = bf16[256,2560]{1,0:T(8,128)(2,1)} collective-permute-done((bf16[256,2560]{1,0:T(8,128)(2,1)}, bf16[256,2560]{1,0:T(8,128)(2,1)}, u32[]{:S(2)}, u32[]{:S(2)}) %collective-permute-start.2) | collective-permute-done | bytes 1310752 | tf_op jit(solution)/shard_map/ppermute | solution.py:9
  82.6 6.2 %collective-permute-start.3 = (bf16[256,2560]{1,0:T(8,128)(2,1)}, bf16[256,2560]{1,0:T(8,128)(2,1)}, u32[]{:S(2)}, u32[]{:S(2)}) collective-permute-start(bf16[256,2560]{1,0:T(8,128)(2,1)} %collective-permute-done.2), channel_id=1, source_target_pairs={{0,480},{32,0},{64,32},{96,64},{128,96},{160,128},{192,160},{224,1... | collective-permute-start | bytes 3932168 | tf_op jit(solution)/shard_map/ppermute | solution.py:9
  88.9 2.4 broadcast.36.clone
  91.3 0.0 copy-done
  91.3 1.2 bitcast_dynamic-update-slice_fusion.4
  92.5 0.1 copy.19
  92.7 2.4 broadcast.36
  95.1 0.7 constant_dynamic-update-slice_fusion.4
  95.8 2.5 bitcast_dynamic-update-slice_fusion.3
  98.4 0.1 copy.20
  98.5 0.7 constant_dynamic-update-slice_fusion.3
  99.2 5.1 %collective-permute-done.3 = bf16[256,2560]{1,0:T(8,128)(2,1)} collective-permute-done((bf16[256,2560]{1,0:T(8,128)(2,1)}, bf16[256,2560]{1,0:T(8,128)(2,1)}, u32[]{:S(2)}, u32[]{:S(2)}) %collective-permute-start.3) | collective-permute-done | bytes 1310752 | tf_op jit(solution)/shard_map/ppermute | solution.py:9
  104.3 6.2 %collective-permute-start.4 = (bf16[256,2560]{1,0:T(8,128)(2,1)}, bf16[256,2560]{1,0:T(8,128)(2,1)S(1)}, u32[]{:S(2)}, u32[]{:S(2)}) collective-permute-start(bf16[256,2560]{1,0:T(8,128)(2,1)} %collective-permute-done.3), channel_id=1, source_target_pairs={{0,480},{32,0},{64,32},{96,64},{128,96},{160,128},{192,160},{224,1... | collective-permute-start | bytes 3932168 | tf_op jit(solution)/shard_map/ppermute | solution.py:9
  110.5 2.6 bitcast_dynamic-update-slice_fusion.2
  113.1 0.1 copy.21
  113.2 0.7 constant_dynamic-update-slice_fusion.2
  113.9 2.6 bitcast_dynamic-update-slice_fusion.1
  116.5 0.1 copy.22
  116.6 0.8 constant_dynamic-update-slice_fusion.1
  117.4 8.5 %collective-permute-done.4 = bf16[256,2560]{1,0:T(8,128)(2,1)S(1)} collective-permute-done((bf16[256,2560]{1,0:T(8,128)(2,1)}, bf16[256,2560]{1,0:T(8,128)(2,1)S(1)}, u32[]{:S(2)}, u32[]{:S(2)}) %collective-permute-start.4) | collective-permute-done | bytes 1310752 | tf_op jit(solution)/shard_map/ppermute | solution.py:9
  125.9 1.3 bitcast_dynamic-update-slice_fusion
  127.2 0.1 copy.23
  127.3 0.7 constant_dynamic-update-slice_fusion
  128.1 5.3 %copy.24 = f32[256,16,256]{2,0,1:T(8,128)} copy(f32[256,16,256]{0,2,1:T(8,128)} %constant_dynamic-update-slice_fusion) | data formatting | bytes 8388608 | tf_op jit(solution)/shard_map/dynamic_update_slice | solution.py:54
  133.4 62.3 %all_to_all.5 = f32[256,16,256]{2,0,1:T(8,128)} all-to-all(f32[256,16,256]{2,0,1:T(8,128)} %copy.24), channel_id=1, replica_groups=mesh['dp'=16,'layer'=16,'rep'=2] {'dp'}, dimensions={1} | all-to-all | bytes 8388608 | tf_op jit(solution)/shard_map/all_to_all | solution.py:57
  195.7 5.3 %copy.25 = f32[256,16,256]{0,2,1:T(8,128)} copy(f32[256,16,256]{2,0,1:T(8,128)} %all_to_all.5) | data formatting | bytes 8388608 | tf_op jit(solution)/shard_map/all_to_all | solution.py:57
  201.1 6.0 %add.104 = f32[256,16,256]{0,2,1:T(8,128)} add(f32[256,16,256]{0,2,1:T(8,128)} %get-tuple-element.13, f32[256,16,256]{0,2,1:T(8,128)} %copy.25) | non-fusion elementwise | flops 1048576 | bytes 12582912 | tf_op jit(solution)/shard_map/add | solution.py:58
  207.1 0.0 reduce-scatter.2.cloned.1.call-update
  207.2 0.3 multiply_reduce_fusion
  207.5 36.5 %psum.7 = f32[256]{0:T(256)S(1)} all-reduce(f32[256]{0:T(256)S(1)} %multiply_reduce_fusion), channel_id=1, replica_groups=mesh['dp'=16,'layer'=16,'rep'=2] {'layer'}, use_global_device_ids=true, to_apply=%region_2.3 | all-reduce | flops 256 | bytes 2048 | tf_op jit(solution)/shard_map/psum | solution.py:21
  244.0 18.8 %all-gather = f32[16,1,256]{2,1,0:T(1,128)S(1)} all-gather(f32[1,1,256]{2,1,0:T(1,128)S(1)} %bitcast.46), channel_id=1, replica_groups=mesh['dp'=16,'layer'=16,'rep'=2] {'dp'}, dimensions={0}, use_global_device_ids=true | all-gather | bytes 17408 | tf_op jit(solution)/shard_map/all_gather | solution.py:22
  262.9 0.1 dynamic_slice.7
  262.9 0.1 dynamic_slice.6
  263.0 91.8 %reduce-scatter.2.cloned.1.call-done = f32[256,128]{0,1:T(8,128)} async-done(((f32[256,4096]{0,1:T(8,128)}), f32[256,128]{0,1:T(8,128)}) %reduce-scatter.2.cloned.1.call-update) | async-done | bytes 131088 | tf_op jit(solution)/shard_map/reduce_scatter | solution.py:59
  354.9 1.0 multiply_multiply_fusion
  355.8 0.8 copy.26
  (6 shorter events, 0.1 us)
Async XLA Ops:
  6.5 348.3 %reduce-scatter.2.cloned.1.call-start = ((), (), s32[]{:S(2)}) async-start(), calls=%async_computation.2 | async-start | bytes 4325376 | tf_op jit(solution)/shard_map/reduce_scatter | solution.py:59
  6.5 34.1 %collective-permute-start = (bf16[256,2560]{1,0:T(8,128)(2,1)}, bf16[256,2560]{1,0:T(8,128)(2,1)S(1)}, u32[]{:S(2)}, u32[]{:S(2)}) collective-permute-start(bf16[256,2560]{1,0:T(8,128)(2,1)} %param.1), channel_id=1, source_target_pairs={{0,256},{32,288},{64,320},{96,352},{128,384},{160,416},{192,448},{... | collective-permute-start | bytes 3932168 | tf_op jit(solution)/shard_map/ppermute | solution.py:9
  42.1 18.8 %collective-permute-start.1 = (bf16[256,2560]{1,0:T(8,128)(2,1)S(1)}, bf16[256,2560]{1,0:T(8,128)(2,1)}, u32[]{:S(2)}, u32[]{:S(2)}) collective-permute-start(bf16[256,2560]{1,0:T(8,128)(2,1)S(1)} %broadcast_select_fusion), channel_id=1, source_target_pairs={{0,480},{32,0},{64,32},{96,64},{128,96},{160,128},{192,160},{224,1... | collective-permute-start | bytes 3932168 | tf_op jit(solution)/shard_map/ppermute | solution.py:9
  60.9 21.7 %collective-permute-start.2 = (bf16[256,2560]{1,0:T(8,128)(2,1)}, bf16[256,2560]{1,0:T(8,128)(2,1)}, u32[]{:S(2)}, u32[]{:S(2)}) collective-permute-start(bf16[256,2560]{1,0:T(8,128)(2,1)} %collective-permute-done.1), channel_id=1, source_target_pairs={{0,480},{32,0},{64,32},{96,64},{128,96},{160,128},{192,160},{224,1... | collective-permute-start | bytes 3932168 | tf_op jit(solution)/shard_map/ppermute | solution.py:9
  67.3 23.9 %copy-start = (bf16[256,2560]{1,0:T(8,128)(2,1)S(1)}, bf16[256,2560]{1,0:T(8,128)(2,1)}, u32[]{:S(2)}) copy-start(bf16[256,2560]{1,0:T(8,128)(2,1)} %param.1) | copy-start | bytes 3932164
  82.6 21.6 %collective-permute-start.3 = (bf16[256,2560]{1,0:T(8,128)(2,1)}, bf16[256,2560]{1,0:T(8,128)(2,1)}, u32[]{:S(2)}, u32[]{:S(2)}) collective-permute-start(bf16[256,2560]{1,0:T(8,128)(2,1)} %collective-permute-done.2), channel_id=1, source_target_pairs={{0,480},{32,0},{64,32},{96,64},{128,96},{160,128},{192,160},{224,1... | collective-permute-start | bytes 3932168 | tf_op jit(solution)/shard_map/ppermute | solution.py:9
  104.3 21.6 %collective-permute-start.4 = (bf16[256,2560]{1,0:T(8,128)(2,1)}, bf16[256,2560]{1,0:T(8,128)(2,1)S(1)}, u32[]{:S(2)}, u32[]{:S(2)}) collective-permute-start(bf16[256,2560]{1,0:T(8,128)(2,1)} %collective-permute-done.3), channel_id=1, source_target_pairs={{0,480},{32,0},{64,32},{96,64},{128,96},{160,128},{192,160},{224,1... | collective-permute-start | bytes 3932168 | tf_op jit(solution)/shard_map/ppermute | solution.py:9
Sparse Core Ops, SparseCore 0:
  207.3 147.5 reduce-scatter.1
where the time goes:
time: 364 us; the launch traced here: 363 us
  waiting for transfers between devices  167 us (46%)
  blocking collectives  118 us (32%)
  starting transfers between devices  25.5 us (7%)
  local copies, waits for them, and re-layouts  20.7 us (6%)
  between operations  13.7 us (4%)
  matrix products  10.2 us (3%)
  other arithmetic  8.92 us (2%)
    reduce_scatter x1, waiting for transfers between devices, body(): lax.psum_scatter(combined, ('layer', 'rep'), scatter_dimension=1, tiled=T...  91.8 us
    ppermute x5, waiting for transfers between devices, from_behind(): lax.ppermute(array, axis, [(i, (i + by) % length) for i in range(length)])  74.9 us
    all_to_all x1, blocking collectives, body(): lax.all_to_all(mirror_tiles, 'dp', split_axis=1, concat_axis=1, tiled=True)  62.3 us
    psum x1, blocking collectives, body(): group_total = lax.psum(squares, 'layer')  36.5 us
    ppermute x5, starting transfers between devices, from_behind(): lax.ppermute(array, axis, [(i, (i + by) % length) for i in range(length)])  25.5 us
    all_gather x1, blocking collectives, body(): norm_values = lax.all_gather(group_total, 'dp', axis=0, tiled=True)  18.8 us
    dot_general x5, matrix products, body(): lax.dot_general(grads, visiting, (((1,), (1,)), ((), ())), preferred_elem...  10.2 us
    dynamic_update_slice x6, local copies, waits for them, and re-layouts, body(): lax.dynamic_update_slice(mirror_tiles, flips[turn][:, None, :], (zero_ind...  8.99 us
  transfers between devices with their start and end apart: 6, of which 6 were waited for; matrix products, arithmetic and copies ran while one was open for 5% of the time, Pallas kernels for 0%

commit v1 on v0

v1 whole, which is shorter than its diff:
```python
import functools

import jax
import jax.numpy as jnp
from jax import lax
from jax.experimental import pallas as pl
from jax.experimental.pallas import tpu as pltpu
from jax.sharding import PartitionSpec as P

MESH = pl.DeviceIdType.MESH
F32 = jnp.float32
BF16 = jnp.bfloat16
FEATURES = 2560
HALF = FEATURES // 2
CODE_SCALE = 32768.0
UP, DOWN, OUT, FAR, OWN, OWN0, OWN1 = range(7)
TILES = (
    (OWN, OWN),
    (OWN0, OWN1),
    (OWN, UP),
    (OWN, DOWN),
    (OWN, OUT),
    (UP, DOWN),
    (UP, OUT),
    (DOWN, OUT),
    (OWN, FAR),
)
TILE_COUNT = len(TILES)
NEAR = TILE_COUNT - 1


def edge_bit(h, y):
    return (h + (3 - y % 4) // 3) % 2


def is_direct(dp, layer, rep, half):
    yd, hd = dp // 4, (dp // 2) % 2
    yl, hl = layer // 4, (layer // 2) % 2
    dh, dy = (hl + hd) % 2, (yl - yd + 4) % 4
    parity = (hd + yd) % 2
    mixed = (half + rep) % 2
    above = edge_bit(hd, yd)
    second = edge_bit(hd, yd + 1)
    below = edge_bit(hd, yd + 3)
    same_column = jnp.where(
        dy == 0,
        jnp.where(mixed == 0, 0, half),
        jnp.where(
            dy == 1,
            (mixed + parity + above) % 2,
            jnp.where(dy == 3, (mixed + parity + below) % 2, (mixed + above + second + 1) % 2),
        ),
    )
    other_column = jnp.where(
        dy == 1,
        (mixed + above) % 2,
        jnp.where(dy == 3, (mixed + below) % 2, (mixed + parity) % 2),
    )
    return jnp.where(dh == 0, same_column, other_column) == 0


def decode(code):
    wide = code.astype(F32)
    size = jnp.abs(wide)
    quarter = lax.rsqrt(lax.rsqrt(jnp.maximum(size, 1e-37)))
    eighth = quarter * lax.rsqrt(quarter) * (1.0 / CODE_SCALE)
    return jnp.where(size < 1e-37, 0.0, jnp.where(wide < 0.0, -eighth, eighth))


def kernel(
    g_ref, out_ref, near, own, part, other, total, paired, code, codes, final, staging,
    squares, norm, near_norm, own_norm, row_scale,
    gather_send, gather_recv, own_send, own_recv, local_sem, far_sem, square_send, square_recv,
    norm_send, norm_recv, core_send, core_recv, pair_send, pair_recv, code_send, code_recv,
    final_send, final_recv,
):
    dp = lax.axis_index("dp")
    z = lax.axis_index("layer")
    r = lax.axis_index("rep")
    y, h, c = dp // 4, (dp // 2) % 2, dp % 2
    parity = (h + y) % 2
    g = (r + parity) % 2
    odd = z % 2

    def device(y_, h_, c_, z_, r_):
        return (4 * ((y_ + 4) % 4) + 2 * (h_ % 2) + c_, (z_ + 16) % 16, r_)

    def remote(src, dst, send, recv, target):
        return pltpu.make_async_remote_copy(
            src_ref=src, dst_ref=dst, send_sem=send, recv_sem=recv, device_id=target, device_id_type=MESH
        )

    barrier = pltpu.get_barrier_semaphore()
    partners = [device(y, h, 1 - c, z, r), device(y, h, c, z, 1 - r), device(y + 2, h, c, z, r)]
    for core in range(2):
        partners += [device(y + 1, h, core, z, r), device(y + 3, h, core, z, r), device(y, h + 1, core, z, 1 - r)]
    for target in partners:
        pl.semaphore_signal(barrier, inc=1, device_id=target, device_id_type=MESH)
    for step in range(1, 16):
        pl.semaphore_signal(barrier, inc=1, device_id=device(y, h, c, z + step, r), device_id_type=MESH)

    wide = g_ref[...].astype(F32)
    local = jnp.sum(wide * wide, axis=1, keepdims=True)
    squares[z] = jnp.broadcast_to(local, (256, 128)).T[0:1, :]

    pl.semaphore_wait(barrier, len(partners) + 15)

    sends = []
    wants = (
        (UP, (r + edge_bit(h, y + 3)) % 2, y + 3, h, r),
        (DOWN, (r + edge_bit(h, y)) % 2, y + 1, h, r),
        (OUT, 1 - r, y, h + 1, 1 - r),
    )
    for slot, half, y_, h_, r_ in wants:
        rows = pl.ds(pl.multiple_of(half * 128, 128), 128)
        for core in range(2):
            sends.append(
                remote(
                    g_ref.at[rows, pl.ds(core * HALF, HALF)],
                    near.at[slot, pl.ds(pl.multiple_of(c * 128, 128), 128)],
                    gather_send.at[slot, core],
                    gather_recv.at[slot, c],
                    device(y_, h_, core, z, r_),
                )
            )
    for copy in sends:
        copy.start()
    square_sends = []
    for step in range(1, 16):
        square_sends.append(
            remote(
                squares.at[z], squares.at[z], square_send.at[step], square_recv.at[z],
                device(y, h, c, z + step, r),
            )
        )
        square_sends[-1].start()
    mine = pl.ds(pl.multiple_of(c * HALF, 128), HALF)
    theirs = pl.ds(pl.multiple_of((1 - c) * HALF, 128), HALF)
    place = pl.ds(pl.multiple_of(c * 128, 128), 128)
    own_sends = []
    own_copies = []
    for half in range(2):
        rows = pl.ds(half * 128, 128)
        own_sends.append(
            remote(
                g_ref.at[rows, theirs], own.at[half, place], own_send.at[half], own_recv.at[half],
                device(y, h, 1 - c, z, r),
            )
        )
        own_copies.append(pltpu.make_async_copy(g_ref.at[rows, mine], own.at[half, place], local_sem.at[half]))
    for copy in own_sends + own_copies:
        copy.start()

    for step in range(1, 16):
        source = (z + step) % 16
        remote(
            squares.at[source], squares.at[source], square_send.at[step], square_recv.at[source],
            device(y, h, c, z + step, r),
        ).wait_recv()
    inverse = lax.rsqrt(jnp.sum(squares[...], axis=0) + 1e-06)
    norm[0] = inverse[:, 0:128]
    norm[1] = inverse[:, 128:256]
    norm_sends = []
    for slot, half, y_, h_, r_ in wants:
        for core in range(2):
            norm_sends.append(
                remote(
                    norm.at[half], near_norm.at[slot, c], norm_send.at[slot, core], norm_recv.at[slot, c],
                    device(y_, h_, core, z, r_),
                )
            )
    for half in range(2):
        own_norm[half, c] = norm[half]
        norm_sends.append(
            remote(
                norm.at[half], own_norm.at[half, c], norm_send.at[4, half], norm_recv.at[4, half],
                device(y, h, 1 - c, z, r),
            )
        )
    for copy in norm_sends:
        copy.start()

    def block(kind):
        if kind == OWN:
            return own[g]
        if kind in (OWN0, OWN1):
            return own[kind - OWN0]
        return near[kind]

    def norms(kind, index):
        if kind == OWN:
            return own_norm[g, index]
        if kind in (OWN0, OWN1):
            return own_norm[kind - OWN0, index]
        return near_norm[kind, index]

    core_sends = []

    def product(tile):
        left, right = TILES[tile]
        value = lax.dot_general(block(left), block(right), (((1,), (1,)), ((), ())), preferred_element_type=F32)
        part[tile, 0] = value[:, 0:128]
        part[tile, 1] = value[:, 128:256]
        core_sends.append(
            remote(
                part.at[tile, 1 - c], other.at[tile], core_send.at[tile], core_recv.at[tile],
                device(y, h, 1 - c, z, r),
            )
        )
        core_sends[-1].start()

    for half in range(2):
        own_copies[half].wait()
        own_sends[half].wait_recv()
    product(0)
    product(1)

    def arrived(slot):
        for core in range(2):
            remote(
                near.at[slot, pl.ds(core * 128, 128)], near.at[slot, pl.ds(core * 128, 128)],
                gather_send.at[slot, core], gather_recv.at[slot, core], device(y, h, 1 - c, z, r),
            ).wait_recv()
            remote(
                near_norm.at[slot, core], near_norm.at[slot, core],
                norm_send.at[slot, core], norm_recv.at[slot, core], device(y, h, 1 - c, z, r),
            ).wait_recv()

    arrived(OUT)
    far_copy = remote(near.at[OUT], near.at[FAR], far_sem.at[0], far_sem.at[1], device(y + 2, h, c, z, r))
    far_copy.start()
    far_norm = remote(near_norm.at[OUT], near_norm.at[FAR], far_sem.at[2], far_sem.at[3], device(y + 2, h, c, z, r))
    far_norm.start()
    arrived(UP)
    arrived(DOWN)
    for half in range(2):
        remote(
            own_norm.at[half, 1 - c], own_norm.at[half, 1 - c], norm_send.at[4, half], norm_recv.at[4, half],
            device(y, h, 1 - c, z, r),
        ).wait_recv()
    for tile in range(2, NEAR):
        product(tile)

    scale_slot = {OWN: 0, OWN0: 1, UP: 2, DOWN: 3}
    for kind, index in scale_slot.items():
        for half in range(2):
            square = jnp.broadcast_to(norms(kind, half), (128, 128)).T * CODE_SCALE
            row_scale[index, 2 * half] = square[0:64]
            row_scale[index, 2 * half + 1] = square[64:128]

    pair_targets = (device(y, h, c, z + 1 - 2 * odd, r), device(y, h, c, z - 1 + 2 * odd, r))

    def pair_copies(first, count, batch):
        copies = []
        for side in range(2):
            copies.append(
                remote(
                    total.at[pl.ds(first, count), 2 * side + 1 - odd], paired.at[side, pl.ds(first, count)],
                    pair_send.at[batch, side], pair_recv.at[batch, side], pair_targets[side],
                )
            )
        return copies

    def join_cores(tile):
        core_sends[tile].wait_recv()
        value = part[tile, c] + other[tile]
        for quarter in range(4):
            total[tile, quarter] = value[64 * quarter : 64 * quarter + 64]

    def encode_tile(tile):
        left, right = TILES[tile]
        columns = norms(right, c)
        for side in range(2):
            quarter = 2 * side + odd
            value = total[tile, quarter] + paired[side, tile]
            scaled = value * row_scale[scale_slot[left], quarter] * columns
            square = scaled * scaled
            coded = (square * square * square * scaled * jnp.abs(scaled)).astype(BF16)
            for j in range(4):
                code[2 * j + side, tile] = coded[16 * j : 16 * j + 16]

    def code_copies(first, count, batch):
        copies = []
        for step in range(1, 8):
            slot = (z // 2 + step) % 8
            copies.append(
                remote(
                    code.at[slot, pl.ds(first, count)], codes.at[z // 2, pl.ds(first, count)],
                    code_send.at[batch, step], code_recv.at[batch, z // 2],
                    device(y, h, c, 2 * slot + odd, r),
                )
            )
        return copies

    def wait_codes(first, count, batch):
        for step in range(1, 8):
            slot = (z // 2 + step) % 8
            remote(
                codes.at[slot, pl.ds(first, count)], codes.at[slot, pl.ds(first, count)],
                code_send.at[batch, step], code_recv.at[batch, slot],
                device(y, h, c, 2 * slot + odd, r),
            ).wait_recv()

    def sum_codes(first, count):
        value = decode(code[z // 2, first : first + count])
        for step in range(1, 8):
            value = value + decode(codes[(z // 2 + step) % 8, first : first + count])
        final[first : first + count] = value

    row_block = (z % 4) // 2
    offset = pl.multiple_of(64 * (z % 2) + 16 * (z // 4), 16)
    strip = pl.ds(offset, 16)
    sets = {
        OWN: (y, h, g),
        OWN0: (y, h, 0),
        OWN1: (y, h, 1),
        UP: (y + 1, h, (r + edge_bit(h, y)) % 2),
        DOWN: (y + 3, h, (r + edge_bit(h, y + 3)) % 2),
        OUT: (y, h + 1, r),
        FAR: (y + 2, h + 1, r),
    }

    def index_of(kind, block_index):
        y_, h_, _ = sets[kind]
        return 4 * ((y_ + 4) % 4) + 2 * (h_ % 2) + block_index

    final_waits = []

    def deliver(tile, number, row, column, rep, half):
        copy = remote(
            final.at[tile], staging.at[half, strip], final_send.at[tile, number], final_recv, (row, column, rep)
        )
        here = jnp.logical_and(jnp.logical_and(row == dp, column == z), rep == r)
        stay = pltpu.make_async_copy(final.at[tile], staging.at[half, strip], final_recv)

        @pl.when(jnp.logical_not(here))
        def _():
            copy.start()

        @pl.when(here)
        def _():
            stay.start()

        final_waits.append((copy, here))

    def deliver_tile(tile):
        left, right = TILES[tile]
        row, column = index_of(left, row_block), index_of(right, c)
        left_set, right_set = sets[left][2], sets[right][2]
        if tile == 0:
            deliver(tile, 0, row, column, right_set, left_set)
        elif tile == 1:
            first = r == 0
            deliver(
                tile, 0, jnp.where(first, row, column), jnp.where(first, column, row),
                jnp.where(first, 1, 0), jnp.where(first, 0, 1),
            )
        else:
            deliver(tile, 0, row, column, right_set, left_set)
            deliver(tile, 1, column, row, left_set, right_set)

    for tile in range(NEAR):
        join_cores(tile)
    pair_first = pair_copies(0, NEAR, 0)
    for copy in pair_first:
        copy.start()
    for copy in pair_first:
        copy.wait_recv()
    for tile in range(NEAR):
        encode_tile(tile)
    codes_first = code_copies(0, NEAR, 0)
    for copy in codes_first:
        copy.start()

    far_copy.wait_recv()
    far_norm.wait_recv()
    product(NEAR)
    join_cores(NEAR)
    pair_second = pair_copies(NEAR, 1, 1)
    for copy in pair_second:
        copy.start()
    for copy in pair_second:
        copy.wait_recv()
    encode_tile(NEAR)
    codes_second = code_copies(NEAR, 1, 1)
    for copy in codes_second:
        copy.start()

    wait_codes(0, NEAR, 0)
    sum_codes(0, NEAR)
    for tile in range(NEAR):
        deliver_tile(tile)
    wait_codes(NEAR, 1, 1)
    sum_codes(NEAR, 1)
    deliver_tile(NEAR)

    pltpu.make_async_copy(staging, staging, final_recv).wait()
    for half in range(2):
        direct = is_direct(dp, z, r, half)

        @pl.when(direct)
        def _():
            out_ref[pl.ds(half * 128, 128), :] = staging[half]

        @pl.when(jnp.logical_not(direct))
        def _():
            out_ref[pl.ds(half * 128, 128), :] = staging[half].T

    waits = sends + square_sends + own_sends + norm_sends + [far_copy, far_norm] + core_sends
    waits += pair_first + pair_second + codes_first + codes_second
    for copy in waits:
        copy.wait_send()
    for copy, here in final_waits:

        @pl.when(jnp.logical_not(here))
        def _():
            copy.wait_send()


def body(grads):
    dma = pltpu.SemaphoreType.DMA
    return pl.pallas_call(
        kernel,
        out_shape=jax.ShapeDtypeStruct((256, 128), F32),
        in_specs=[pl.BlockSpec(memory_space=pltpu.VMEM)],
        out_specs=pl.BlockSpec(memory_space=pltpu.VMEM),
        scratch_shapes=[
            pltpu.VMEM((4, 256, HALF), BF16),
            pltpu.VMEM((2, 256, HALF), BF16),
            pltpu.VMEM((TILE_COUNT, 2, 256, 128), F32),
            pltpu.VMEM((TILE_COUNT, 256, 128), F32),
            pltpu.VMEM((TILE_COUNT, 4, 64, 128), F32),
            pltpu.VMEM((2, TILE_COUNT, 64, 128), F32),
            pltpu.VMEM((8, TILE_COUNT, 16, 128), BF16),
            pltpu.VMEM((8, TILE_COUNT, 16, 128), BF16),
            pltpu.VMEM((TILE_COUNT, 16, 128), F32),
            pltpu.VMEM((2, 128, 128), F32),
            pltpu.VMEM((16, 1, 256), F32),
            pltpu.VMEM((2, 1, 128), F32),
            pltpu.VMEM((4, 2, 1, 128), F32),
            pltpu.VMEM((2, 2, 1, 128), F32),
            pltpu.VMEM((4, 4, 64, 128), F32),
            dma((3, 2)),
            dma((3, 2)),
            dma((2,)),
            dma((2,)),
            dma((2,)),
            dma((4,)),
            dma((16,)),
            dma((16,)),
            dma((5, 2)),
            dma((5, 2)),
            dma((TILE_COUNT,)),
            dma((TILE_COUNT,)),
            dma((2, 2)),
            dma((2, 2)),
            dma((2, 8)),
            dma((2, 8)),
            dma((TILE_COUNT, 2)),
            dma,
        ],
        compiler_params=pltpu.CompilerParams(
            collective_id=0, has_side_effects=True, vmem_limit_bytes=40 * 1024 * 1024
        ),
        cost_estimate=pl.CostEstimate(flops=1510000000, bytes_accessed=1500000, transcendentals=0),
    )(grads)


def solution(mesh):
    in_specs = (P("dp", "layer"),)
    out_specs = P("dp", ("layer", "rep"))
    return jax.shard_map(body, mesh=mesh, in_specs=in_specs, out_specs=out_specs, check_vma=False)
```

time: 364 us -> 84.7 us (0.23)
  the two profiles are of different devices: /device:TPU:24 before, /device:TPU:22 now
where the time goes in v1:
time: 84.7 us; the launch traced here: 84.6 us
  Pallas kernels  82.6 us (98%)
  local copies, waits for them, and re-layouts  1.97 us (2%)
    pallas_call x1, Pallas kernels, body(): pl.pallas_call(kernel, out_shape=jax.ShapeDtypeStruct((256, 128), F32), i...  82.6 us
    unnamed x3, local copies, waits for them, and re-layouts  1.97 us

profile of v1, /device:TPU:22, one launch (start us, length us, event | category | flops | bytes accessed | tf_op | source)
XLA Modules:
  0.0 84.6 jit_solution(9866089761400906957)
XLA Ops:
  0.0 0.0 copy-start
  0.0 1.3 %copy-done = bf16[256,2560]{1,0:T(8,128)(2,1)S(1)} copy-done((bf16[256,2560]{1,0:T(8,128)(2,1)S(1)}, bf16[256,2560]{1,0:T(8,128)(2,1)}, u32[]{:S(2)}) %copy-start) | copy-done | bytes 1310744
  1.3 82.6 %shard_map.17 = f32[256,128]{1,0:T(8,128)S(1)} custom-call(bf16[256,2560]{1,0:T(8,128)(2,1)S(1)} %copy-done), custom_call_target="tpu_custom_call" | custom-call | flops 1510000000 | bytes 1500000 | tf_op jit(solution)/shard_map/pallas_call | solution.py:422
  83.9 0.7 copy.3
Async XLA Ops:
  0.0 1.3 %copy-start = (bf16[256,2560]{1,0:T(8,128)(2,1)S(1)}, bf16[256,2560]{1,0:T(8,128)(2,1)}, u32[]{:S(2)}) copy-start(bf16[256,2560]{1,0:T(8,128)(2,1)} %g_ref.1) | copy-start | bytes 3932164

commit v2 on v1

v2 whole, which is shorter than its diff:
```python
import functools

import jax
import jax.numpy as jnp
from jax import lax
from jax.experimental import pallas as pl
from jax.experimental.pallas import tpu as pltpu
from jax.sharding import PartitionSpec as P

MESH = pl.DeviceIdType.MESH
F32 = jnp.float32
BF16 = jnp.bfloat16
FEATURES = 2560
HALF = FEATURES // 2
CODE_SCALE = 32768.0
UP, DOWN, OUT, FAR, OWN, OWN0, OWN1, LAST = range(8)
TILES = (
    (OWN, OWN),
    (OWN0, OWN1),
    (OWN, UP),
    (OWN, DOWN),
    (UP, DOWN),
    (UP, OUT),
    (DOWN, OUT),
    (OWN0, LAST),
    (OWN1, LAST),
)
TILE_COUNT = len(TILES)
BATCHES = ((0, 2), (2, 5), (7, 2))


def edge_bit(h, y):
    return (h + (3 - y % 4) // 3) % 2


def is_direct(dp, layer, rep, half):
    yd, hd = dp // 4, (dp // 2) % 2
    yl, hl = layer // 4, (layer // 2) % 2
    dh, dy = (hl + hd) % 2, (yl - yd + 4) % 4
    parity = (hd + yd) % 2
    mixed = (half + rep) % 2
    above = edge_bit(hd, yd)
    second = edge_bit(hd, yd + 1)
    below = edge_bit(hd, yd + 3)
    same_column = jnp.where(
        dy == 0,
        jnp.where(mixed == 0, 0, half),
        jnp.where(
            dy == 1,
            (mixed + parity + above) % 2,
            jnp.where(dy == 3, (mixed + parity + below) % 2, (mixed + above + second + 1) % 2),
        ),
    )
    other_column = jnp.where(
        dy == 1,
        (mixed + above) % 2,
        jnp.where(dy == 3, (mixed + below) % 2, jnp.where(dy == 0, 1 - parity, parity)),
    )
    return jnp.where(dh == 0, same_column, other_column) == 0


def decode(code):
    wide = code.astype(F32)
    size = jnp.abs(wide)
    quarter = lax.rsqrt(lax.rsqrt(jnp.maximum(size, 1e-37)))
    eighth = quarter * lax.rsqrt(quarter) * (1.0 / CODE_SCALE)
    return jnp.where(size < 1e-37, 0.0, jnp.where(wide < 0.0, -eighth, eighth))


def kernel(
    g_ref, out_ref, near, own, part, other, total, paired, code, codes, final, staging,
    squares, norm, near_norm, own_norm, row_scale,
    gather_send, gather_recv, own_send, own_recv, local_sem, far_sem, square_send, square_recv,
    norm_send, norm_recv, core_send, core_recv, pair_send, pair_recv, code_send, code_recv,
    final_send, final_recv,
):
    dp = lax.axis_index("dp")
    z = lax.axis_index("layer")
    r = lax.axis_index("rep")
    y, h, c = dp // 4, (dp // 2) % 2, dp % 2
    parity = (h + y) % 2
    g = (r + parity) % 2
    odd = z % 2
    even_chip = parity == 0
    last_slot = OUT + 1 - parity

    def device(y_, h_, c_, z_, r_):
        return (4 * ((y_ + 4) % 4) + 2 * (h_ % 2) + c_, (z_ + 16) % 16, r_)

    def remote(src, dst, send, recv, target):
        return pltpu.make_async_remote_copy(
            src_ref=src, dst_ref=dst, send_sem=send, recv_sem=recv, device_id=target, device_id_type=MESH
        )

    barrier = pltpu.get_barrier_semaphore()
    partners = [device(y, h, 1 - c, z, r), device(y, h, c, z, 1 - r), device(y + 2, h, c, z, r)]
    for core in range(2):
        partners += [device(y + 1, h, core, z, r), device(y + 3, h, core, z, r), device(y, h + 1, core, z, 1 - r)]
    for target in partners:
        pl.semaphore_signal(barrier, inc=1, device_id=target, device_id_type=MESH)
    for step in range(1, 16):
        pl.semaphore_signal(barrier, inc=1, device_id=device(y, h, c, z + step, r), device_id_type=MESH)

    wide = g_ref[...].astype(F32)
    local = jnp.sum(wide * wide, axis=1, keepdims=True)
    squares[z] = jnp.broadcast_to(local, (256, 128)).T[0:1, :]

    pl.semaphore_wait(barrier, len(partners) + 15)

    sends = []
    wants = (
        (UP, (r + edge_bit(h, y + 3)) % 2, y + 3, h, r),
        (DOWN, (r + edge_bit(h, y)) % 2, y + 1, h, r),
        (OUT, 1 - r, y, h + 1, 1 - r),
    )
    for slot, half, y_, h_, r_ in wants:
        rows = pl.ds(pl.multiple_of(half * 128, 128), 128)
        for core in range(2):
            sends.append(
                remote(
                    g_ref.at[rows, pl.ds(core * HALF, HALF)],
                    near.at[slot, pl.ds(pl.multiple_of(c * 128, 128), 128)],
                    gather_send.at[slot, core],
                    gather_recv.at[slot, c],
                    device(y_, h_, core, z, r_),
                )
            )
    for copy in sends:
        copy.start()
    square_sends = []
    for step in range(1, 16):
        square_sends.append(
            remote(
                squares.at[z], squares.at[z], square_send.at[step], square_recv.at[z],
                device(y, h, c, z + step, r),
            )
        )
        square_sends[-1].start()
    mine = pl.ds(pl.multiple_of(c * HALF, 128), HALF)
    theirs = pl.ds(pl.multiple_of((1 - c) * HALF, 128), HALF)
    place = pl.ds(pl.multiple_of(c * 128, 128), 128)
    own_sends = []
    own_copies = []
    for half in range(2):
        rows = pl.ds(half * 128, 128)
        own_sends.append(
            remote(
                g_ref.at[rows, theirs], own.at[half, place], own_send.at[half], own_recv.at[half],
                device(y, h, 1 - c, z, r),
            )
        )
        own_copies.append(pltpu.make_async_copy(g_ref.at[rows, mine], own.at[half, place], local_sem.at[half]))
    for copy in own_sends + own_copies:
        copy.start()

    def block(kind):
        if kind == OWN:
            return own[g]
        if kind in (OWN0, OWN1):
            return own[kind - OWN0]
        if kind == LAST:
            return near[last_slot]
        return near[kind]

    def norms(kind, index):
        if kind == OWN:
            return own_norm[g, index]
        if kind in (OWN0, OWN1):
            return own_norm[kind - OWN0, index]
        if kind == LAST:
            return near_norm[last_slot, index]
        return near_norm[kind, index]

    core_sends = []

    def product(tile):
        left, right = TILES[tile]
        value = lax.dot_general(block(left), block(right), (((1,), (1,)), ((), ())), preferred_element_type=F32)
        part[tile, 0] = value[:, 0:128]
        part[tile, 1] = value[:, 128:256]
        core_sends.append(
            remote(
                part.at[tile, 1 - c], other.at[tile], core_send.at[tile], core_recv.at[tile],
                device(y, h, 1 - c, z, r),
            )
        )
        core_sends[-1].start()

    def join_cores(tile):
        core_sends[tile].wait_recv()
        value = part[tile, c] + other[tile]
        for quarter in range(4):
            total[tile, quarter] = value[64 * quarter : 64 * quarter + 64]

    scale_slot = {OWN: 0, OWN0: 1, OWN1: 2, UP: 3, DOWN: 4}

    def spread_norms(kind):
        for half in range(2):
            square = jnp.broadcast_to(norms(kind, half), (128, 128)).T * CODE_SCALE
            row_scale[scale_slot[kind], 2 * half] = square[0:64]
            row_scale[scale_slot[kind], 2 * half + 1] = square[64:128]

    pair_targets = (device(y, h, c, z + 1 - 2 * odd, r), device(y, h, c, z - 1 + 2 * odd, r))

    def pair_copies(batch):
        first, count = BATCHES[batch]
        return [
            remote(
                total.at[pl.ds(first, count), 2 * side + 1 - odd], paired.at[side, pl.ds(first, count)],
                pair_send.at[batch, side], pair_recv.at[batch, side], pair_targets[side],
            )
            for side in range(2)
        ]

    def encode_tile(tile):
        left, right = TILES[tile]
        columns = norms(right, c)
        for side in range(2):
            quarter = 2 * side + odd
            value = total[tile, quarter] + paired[side, tile]
            scaled = value * row_scale[scale_slot[left], quarter] * columns
            square = scaled * scaled
            coded = (square * square * square * scaled * jnp.abs(scaled)).astype(BF16)
            for j in range(4):
                code[2 * j + side, tile] = coded[16 * j : 16 * j + 16]

    def code_copies(batch):
        first, count = BATCHES[batch]
        copies = []
        for step in range(1, 8):
            slot = (z // 2 + step) % 8
            copies.append(
                remote(
                    code.at[slot, pl.ds(first, count)], codes.at[z // 2, pl.ds(first, count)],
                    code_send.at[batch, step], code_recv.at[batch, z // 2],
                    device(y, h, c, 2 * slot + odd, r),
                )
            )
        return copies

    def wait_codes(batch):
        first, count = BATCHES[batch]
        for step in range(1, 8):
            slot = (z // 2 + step) % 8
            remote(
                codes.at[slot, pl.ds(first, count)], codes.at[slot, pl.ds(first, count)],
                code_send.at[batch, step], code_recv.at[batch, slot],
                device(y, h, c, 2 * slot + odd, r),
            ).wait_recv()

    def sum_codes(batch):
        first, count = BATCHES[batch]
        value = decode(code[z // 2, first : first + count])
        for step in range(1, 8):
            value = value + decode(codes[(z // 2 + step) % 8, first : first + count])
        final[first : first + count] = value

    row_block = (z % 4) // 2
    offset = pl.multiple_of(64 * (z % 2) + 16 * (z // 4), 16)
    strip = pl.ds(offset, 16)
    sets = {
        OWN: (y, h, g),
        OWN0: (y, h, 0),
        OWN1: (y, h, 1),
        UP: (y + 1, h, (r + edge_bit(h, y)) % 2),
        DOWN: (y + 3, h, (r + edge_bit(h, y + 3)) % 2),
        OUT: (y, h + 1, r),
        LAST: (y + 2 * (1 - parity), h + 1, r),
    }

    def index_of(kind, block_index):
        y_, h_, _ = sets[kind]
        return 4 * ((y_ + 4) % 4) + 2 * (h_ % 2) + block_index

    final_waits = []

    def deliver(tile, number, row, column, rep, half):
        copy = remote(
            final.at[tile], staging.at[half, strip], final_send.at[tile, number], final_recv, (row, column, rep)
        )
        here = jnp.logical_and(jnp.logical_and(row == dp, column == z), rep == r)
        stay = pltpu.make_async_copy(final.at[tile], staging.at[half, strip], final_recv)

        @pl.when(jnp.logical_not(here))
        def _():
            copy.start()

        @pl.when(here)
        def _():
            stay.start()

        final_waits.append((copy, here))

    def deliver_tile(tile):
        left, right = TILES[tile]
        row, column = index_of(left, row_block), index_of(right, c)
        left_set, right_set = sets[left][2], sets[right][2]
        if tile == 0:
            deliver(tile, 0, row, column, right_set, left_set)
        elif tile == 1:
            first = r == 0
            deliver(
                tile, 0, jnp.where(first, row, column), jnp.where(first, column, row),
                jnp.where(first, 1, 0), jnp.where(first, 0, 1),
            )
        else:
            deliver(tile, 0, row, column, right_set, left_set)
            deliver(tile, 1, column, row, left_set, right_set)

    def tiles_of(batch):
        first, count = BATCHES[batch]
        return range(first, first + count)

    def finish_batch(batch):
        wait_codes(batch)
        sum_codes(batch)
        for tile in tiles_of(batch):
            deliver_tile(tile)

    pairs = [pair_copies(batch) for batch in range(3)]
    code_sends = [code_copies(batch) for batch in range(3)]

    def start_pairs(batch):
        for tile in tiles_of(batch):
            join_cores(tile)
        for copy in pairs[batch]:
            copy.start()

    def start_codes(batch):
        for copy in pairs[batch]:
            copy.wait_recv()
        for tile in tiles_of(batch):
            encode_tile(tile)
        for copy in code_sends[batch]:
            copy.start()

    for half in range(2):
        own_copies[half].wait()
        own_sends[half].wait_recv()
    for tile in tiles_of(0):
        product(tile)

    for step in range(1, 16):
        source = (z + step) % 16
        remote(
            squares.at[source], squares.at[source], square_send.at[step], square_recv.at[source],
            device(y, h, c, z + step, r),
        ).wait_recv()
    inverse = lax.rsqrt(jnp.sum(squares[...], axis=0) + 1e-06)
    norm[0] = inverse[:, 0:128]
    norm[1] = inverse[:, 128:256]
    norm_sends = []
    for slot, half, y_, h_, r_ in wants:
        for core in range(2):
            norm_sends.append(
                remote(
                    norm.at[half], near_norm.at[slot, c], norm_send.at[slot, core], norm_recv.at[slot, c],
                    device(y_, h_, core, z, r_),
                )
            )
    for half in range(2):
        own_norm[half, c] = norm[half]
        norm_sends.append(
            remote(
                norm.at[half], own_norm.at[half, c], norm_send.at[4, half], norm_recv.at[4, half],
                device(y, h, 1 - c, z, r),
            )
        )
    for copy in norm_sends:
        copy.start()

    start_pairs(0)
    for half in range(2):
        remote(
            own_norm.at[half, 1 - c], own_norm.at[half, 1 - c], norm_send.at[4, half], norm_recv.at[4, half],
            device(y, h, 1 - c, z, r),
        ).wait_recv()
    for kind in (OWN, OWN0, OWN1):
        spread_norms(kind)
    start_codes(0)

    def arrived(slot):
        for core in range(2):
            remote(
                near_norm.at[slot, core], near_norm.at[slot, core],
                norm_send.at[slot, core], norm_recv.at[slot, core], device(y, h, 1 - c, z, r),
            ).wait_recv()
            remote(
                near.at[slot, pl.ds(core * 128, 128)], near.at[slot, pl.ds(core * 128, 128)],
                gather_send.at[slot, core], gather_recv.at[slot, core], device(y, h, 1 - c, z, r),
            ).wait_recv()

    arrived(OUT)
    far_copy = remote(near.at[OUT], near.at[FAR], far_sem.at[0], far_sem.at[1], device(y + 2, h, c, z, r))
    far_norm = remote(near_norm.at[OUT], near_norm.at[FAR], far_sem.at[2], far_sem.at[3], device(y + 2, h, c, z, r))

    @pl.when(even_chip)
    def _():
        far_copy.start()
        far_norm.start()

    arrived(UP)
    arrived(DOWN)
    for tile in tiles_of(1):
        product(tile)
    for kind in (UP, DOWN):
        spread_norms(kind)
    start_pairs(1)
    finish_batch(0)
    start_codes(1)

    @pl.when(even_chip)
    def _():
        far_copy.wait_recv()
        far_norm.wait_recv()

    for tile in tiles_of(2):
        product(tile)
    start_pairs(2)
    finish_batch(1)
    start_codes(2)
    finish_batch(2)

    pltpu.make_async_copy(staging, staging, final_recv).wait()
    for half in range(2):
        direct = is_direct(dp, z, r, half)

        @pl.when(direct)
        def _():
            out_ref[pl.ds(half * 128, 128), :] = staging[half]

        @pl.when(jnp.logical_not(direct))
        def _():
            out_ref[pl.ds(half * 128, 128), :] = staging[half].T

    waits = sends + square_sends + own_sends + norm_sends + core_sends
    for batch in range(3):
        waits += pairs[batch] + code_sends[batch]
    for copy in waits:
        copy.wait_send()

    @pl.when(even_chip)
    def _():
        far_copy.wait_send()
        far_norm.wait_send()

    for copy, here in final_waits:

        @pl.when(jnp.logical_not(here))
        def _():
            copy.wait_send()


def body(grads):
    dma = pltpu.SemaphoreType.DMA
    return pl.pallas_call(
        kernel,
        out_shape=jax.ShapeDtypeStruct((256, 128), F32),
        in_specs=[pl.BlockSpec(memory_space=pltpu.VMEM)],
        out_specs=pl.BlockSpec(memory_space=pltpu.VMEM),
        scratch_shapes=[
            pltpu.VMEM((4, 256, HALF), BF16),
            pltpu.VMEM((2, 256, HALF), BF16),
            pltpu.VMEM((TILE_COUNT, 2, 256, 128), F32),
            pltpu.VMEM((TILE_COUNT, 256, 128), F32),
            pltpu.VMEM((TILE_COUNT, 4, 64, 128), F32),
            pltpu.VMEM((2, TILE_COUNT, 64, 128), F32),
            pltpu.VMEM((8, TILE_COUNT, 16, 128), BF16),
            pltpu.VMEM((8, TILE_COUNT, 16, 128), BF16),
            pltpu.VMEM((TILE_COUNT, 16, 128), F32),
            pltpu.VMEM((2, 128, 128), F32),
            pltpu.VMEM((16, 1, 256), F32),
            pltpu.VMEM((2, 1, 128), F32),
            pltpu.VMEM((4, 2, 1, 128), F32),
            pltpu.VMEM((2, 2, 1, 128), F32),
            pltpu.VMEM((5, 4, 64, 128), F32),
            dma((3, 2)),
            dma((3, 2)),
            dma((2,)),
            dma((2,)),
            dma((2,)),
            dma((4,)),
            dma((16,)),
            dma((16,)),
            dma((5, 2)),
            dma((5, 2)),
            dma((TILE_COUNT,)),
            dma((TILE_COUNT,)),
            dma((3, 2)),
            dma((3, 2)),
            dma((3, 8)),
            dma((3, 8)),
            dma((TILE_COUNT, 2)),
            dma,
        ],
        compiler_params=pltpu.CompilerParams(
            collective_id=0, has_side_effects=True, vmem_limit_bytes=40 * 1024 * 1024
        ),
        cost_estimate=pl.CostEstimate(flops=1510000000, bytes_accessed=1500000, transcendentals=0),
    )(grads)


def solution(mesh):
    in_specs = (P("dp", "layer"),)
    out_specs = P("dp", ("layer", "rep"))
    return jax.shard_map(body, mesh=mesh, in_specs=in_specs, out_specs=out_specs, check_vma=False)
```

time: 84.7 us -> 77.9 us (0.920)
  Pallas kernels: 82.6 us -> 75.7 us
    pallas_call x1, Pallas kernels: 82.6 us -> 75.7 us  [body(): pl.pallas_call(kernel, out_shape=jax.ShapeDtypeStruct((256, 128), F32), i...]
where the time goes in v2:
time: 77.9 us; the launch traced here: 77.7 us
  Pallas kernels  75.7 us (97%)
  local copies, waits for them, and re-layouts  1.97 us (3%)
    pallas_call x1, Pallas kernels, body(): pl.pallas_call(kernel, out_shape=jax.ShapeDtypeStruct((256, 128), F32), i...  75.7 us
    unnamed x3, local copies, waits for them, and re-layouts  1.97 us

profile of v2, /device:TPU:22, one launch (start us, length us, event | category | flops | bytes accessed | tf_op | source)
XLA Modules:
  0.0 77.7 jit_solution(2940876287308302914)
XLA Ops:
  0.0 0.0 copy-start
  0.0 1.3 %copy-done = bf16[256,2560]{1,0:T(8,128)(2,1)S(1)} copy-done((bf16[256,2560]{1,0:T(8,128)(2,1)S(1)}, bf16[256,2560]{1,0:T(8,128)(2,1)}, u32[]{:S(2)}) %copy-start) | copy-done | bytes 1310744
  1.3 75.7 %shard_map.17 = f32[256,128]{1,0:T(8,128)S(1)} custom-call(bf16[256,2560]{1,0:T(8,128)(2,1)S(1)} %copy-done), custom_call_target="tpu_custom_call" | custom-call | flops 1510000000 | bytes 1500000 | tf_op jit(solution)/shard_map/pallas_call | solution.py:456
  77.1 0.7 copy.3
Async XLA Ops:
  0.0 1.3 %copy-start = (bf16[256,2560]{1,0:T(8,128)(2,1)S(1)}, bf16[256,2560]{1,0:T(8,128)(2,1)}, u32[]{:S(2)}) copy-start(bf16[256,2560]{1,0:T(8,128)(2,1)} %g_ref.1) | copy-start | bytes 3932164

commit v3 on v2

v3 whole, which is shorter than its diff:
```python
import functools

import jax
import jax.numpy as jnp
from jax import lax
from jax.experimental import pallas as pl
from jax.experimental.pallas import tpu as pltpu
from jax.sharding import PartitionSpec as P

MESH = pl.DeviceIdType.MESH
F32 = jnp.float32
BF16 = jnp.bfloat16
FEATURES = 2560
HALF = FEATURES // 2
CODE_SHIFT = 2.0**-7.5
CODE_SCALE = 13.4
UP, DOWN, OUT, FAR, OWN0, OWN1 = range(6)
TILE_COUNT = 9
BATCHES = ((0, 2), (2, 2), (4, 3), (7, 2))


def edge_bit(h, y):
    return (h + (3 - y % 4) // 3) % 2


def is_direct(dp, layer, rep, half):
    yd, hd = dp // 4, (dp // 2) % 2
    yl, hl = layer // 4, (layer // 2) % 2
    dh, dy = (hl + hd) % 2, (yl - yd + 4) % 4
    parity = (hd + yd) % 2
    mixed = (half + rep) % 2
    above = edge_bit(hd, yd)
    second = edge_bit(hd, yd + 1)
    below = edge_bit(hd, yd + 3)
    same_column = jnp.where(
        dy == 0,
        jnp.where(mixed == 0, 0, half),
        jnp.where(
            dy == 1,
            (mixed + parity + above) % 2,
            jnp.where(dy == 3, (mixed + parity + below) % 2, (mixed + above + second + 1) % 2),
        ),
    )
    other_column = jnp.where(
        dy == 1,
        (mixed + above) % 2,
        jnp.where(dy == 3, (mixed + below) % 2, jnp.where(dy == 0, 1 - parity, parity)),
    )
    return jnp.where(dh == 0, same_column, other_column) == 0


def encode(value):
    power = jnp.abs(value) * CODE_SCALE + CODE_SHIFT * CODE_SCALE
    for _ in range(5):
        power = power * power
    return jnp.where(value == 0.0, 0.0, jnp.where(value < 0.0, -power, power)).astype(BF16)


def decode(code):
    wide = code.astype(F32)
    size = jnp.abs(wide)
    root = jnp.maximum(size, 1e-37)
    for _ in range(4):
        root = lax.rsqrt(root)
    value = root * lax.rsqrt(root) * (1.0 / CODE_SCALE) - CODE_SHIFT
    return jnp.where(size < 1e-37, 0.0, jnp.where(wide < 0.0, -value, value))


def kernel(
    grads_ref, out_ref, g_ref, near, part, other, total, pair_code, paired, code, codes, final, staging,
    squares, norm, near_norm, row_scale,
    gather_send, gather_recv, own_send, own_recv, local_sem, far_sem, square_send, square_recv,
    norm_send, norm_recv, core_send, core_recv, pair_send, pair_recv, code_send, code_recv,
    final_send, final_recv, load_sem,
):
    dp = lax.axis_index("dp")
    z = lax.axis_index("layer")
    r = lax.axis_index("rep")
    y, h, c = dp // 4, (dp // 2) % 2, dp % 2
    parity = (h + y) % 2
    g = (r + parity) % 2
    odd = z % 2
    even_chip = parity == 0
    last_slot = OUT + 1 - parity

    def device(y_, h_, c_, z_, r_):
        return (4 * ((y_ + 4) % 4) + 2 * (h_ % 2) + c_, (z_ + 16) % 16, r_)

    def remote(src, dst, send, recv, target):
        return pltpu.make_async_remote_copy(
            src_ref=src, dst_ref=dst, send_sem=send, recv_sem=recv, device_id=target, device_id_type=MESH
        )

    load = pltpu.make_async_copy(grads_ref, g_ref, load_sem)
    load.start()

    barrier = pltpu.get_barrier_semaphore()
    partners = [device(y, h, 1 - c, z, r), device(y, h, c, z, 1 - r), device(y + 2, h, c, z, r)]
    partners += [device(y + 1, h + 1, c, z, 1 - r), device(y + 3, h + 1, c, z, 1 - r)]
    for core in range(2):
        partners += [device(y + 1, h, core, z, r), device(y + 3, h, core, z, r), device(y, h + 1, core, z, 1 - r)]
    for target in partners:
        pl.semaphore_signal(barrier, inc=1, device_id=target, device_id_type=MESH)
    for step in range(1, 16):
        pl.semaphore_signal(barrier, inc=1, device_id=device(y, h, c, z + step, r), device_id_type=MESH)

    load.wait()

    @pl.loop(0, 8)
    def _(group):
        wide = g_ref[pl.ds(pl.multiple_of(group * 32, 32), 32), :].astype(F32)
        local = jnp.sum(wide * wide, axis=1, keepdims=True)
        row_scale[0, pl.ds(pl.multiple_of(group * 32, 32), 32)] = jnp.broadcast_to(local, (32, 128))

    squares[z] = row_scale[0].T[0:1, :]

    pl.semaphore_wait(barrier, len(partners) + 15)

    wants = (
        (UP, (r + edge_bit(h, y + 3)) % 2, y + 3, h, r),
        (DOWN, (r + edge_bit(h, y)) % 2, y + 1, h, r),
        (OUT, 1 - r, y, h + 1, 1 - r),
    )
    def gather_copies(slot, half, y_, h_, r_):
        rows = pl.ds(pl.multiple_of(half * 128, 128), 128)
        return [
            remote(
                g_ref.at[rows, pl.ds(core * HALF, HALF)],
                near.at[slot, pl.ds(pl.multiple_of(c * 128, 128), 128)],
                gather_send.at[slot, core],
                gather_recv.at[slot, c],
                device(y_, h_, core, z, r_),
            )
            for core in range(2)
        ]

    gather = [copy for want in wants for copy in gather_copies(*want)]
    for copy in gather:
        copy.start()
    square_sends = []
    for step in range(1, 16):
        square_sends.append(
            remote(
                squares.at[z], squares.at[z], square_send.at[step], square_recv.at[z],
                device(y, h, c, z + step, r),
            )
        )
        square_sends[-1].start()
    mine = pl.ds(pl.multiple_of(c * HALF, 128), HALF)
    theirs = pl.ds(pl.multiple_of((1 - c) * HALF, 128), HALF)
    place = pl.ds(pl.multiple_of(c * 128, 128), 128)
    own_sends = []
    own_copies = []
    for half in range(2):
        rows = pl.ds(half * 128, 128)
        own_sends.append(
            remote(
                g_ref.at[rows, theirs], near.at[OWN0 + half, place], own_send.at[half], own_recv.at[half],
                device(y, h, 1 - c, z, r),
            )
        )
        own_copies.append(pltpu.make_async_copy(g_ref.at[rows, mine], near.at[OWN0 + half, place], local_sem.at[half]))
    for copy in own_sends + own_copies:
        copy.start()

    def choose(tile, values):
        chosen = values[-1]
        for index in range(len(values) - 2, -1, -1):
            chosen = jnp.where(tile == index, values[index], chosen)
        return chosen

    own = OWN0 + g

    def slots(tile):
        left = choose(tile, (own, OWN0, own, own, UP, UP, DOWN, OWN0, OWN1))
        right = choose(tile, (own, OWN1, UP, DOWN, DOWN, OUT, OUT, last_slot, last_slot))
        return left, right

    def core_copy(tile):
        return remote(
            part.at[tile, 1 - c], other.at[tile], core_send.at[tile], core_recv.at[tile], device(y, h, 1 - c, z, r)
        )

    def over_tiles(batch, step):
        first, count = BATCHES[batch]
        pl.loop(first, first + count)(step)

    def product(tile):
        left, right = slots(tile)
        value = lax.dot_general(near[left], near[right], (((1,), (1,)), ((), ())), preferred_element_type=F32)
        part[tile, 0] = value[:, 0:128]
        part[tile, 1] = value[:, 128:256]
        core_copy(tile).start()

    pair_targets = (device(y, h, c, z + 1 - 2 * odd, r), device(y, h, c, z - 1 + 2 * odd, r))

    def pair_copy(side, tile):
        return remote(
            pair_code.at[side, tile], paired.at[side, tile], pair_send.at[tile, side], pair_recv.at[tile, side],
            pair_targets[side],
        )

    def join_cores(tile):
        left, right = slots(tile)
        core_copy(tile).wait_recv()
        value = (part[tile, c] + other[tile]) * row_scale[left] * near_norm[right, c]
        total[tile] = value.reshape(4, 64, 128)
        for side in range(2):
            pair_code[side, tile] = encode(total[tile, 2 * side + 1 - odd])
            pair_copy(side, tile).start()

    def spread_norms(slot):
        for half in range(2):
            row_scale[slot, pl.ds(128 * half, 128)] = jnp.broadcast_to(near_norm[slot, half], (128, 128)).T

    def encode_tile(tile):
        for side in range(2):
            pair_copy(side, tile).wait_recv()
            coded = encode(total[tile, 2 * side + odd] + decode(paired[side, tile]))
            for j in range(4):
                code[2 * j + side, tile] = coded[16 * j : 16 * j + 16]

    def code_copies(batch):
        first, count = BATCHES[batch]
        copies = []
        for step in range(1, 8):
            slot = (z // 2 + step) % 8
            copies.append(
                remote(
                    code.at[slot, pl.ds(first, count)], codes.at[z // 2, pl.ds(first, count)],
                    code_send.at[batch, step], code_recv.at[batch, z // 2],
                    device(y, h, c, 2 * slot + odd, r),
                )
            )
        return copies

    def wait_codes(batch):
        first, count = BATCHES[batch]
        for step in range(1, 8):
            slot = (z // 2 + step) % 8
            remote(
                codes.at[slot, pl.ds(first, count)], codes.at[slot, pl.ds(first, count)],
                code_send.at[batch, step], code_recv.at[batch, slot],
                device(y, h, c, 2 * slot + odd, r),
            ).wait_recv()

    def sum_codes(tile):
        def add(step, value):
            return value + decode(codes[(z // 2 + step) % 8, tile])

        final[tile] = encode(lax.fori_loop(1, 8, add, decode(code[z // 2, tile])))

    row_block = (z % 4) // 2
    offset = pl.multiple_of(64 * (z % 2) + 16 * (z // 4), 16)
    strip = pl.ds(offset, 16)
    def places(slot):
        y_ = choose(slot, (y + 1, y + 3, y, y + 2, y, y))
        h_ = choose(slot, (h, h, h + 1, h + 1, h, h))
        far_set = jnp.where(c == 1, (1 - r + edge_bit(h + 1, y + 1)) % 2, r)
        set_ = choose(slot, ((r + edge_bit(h, y)) % 2, (r + edge_bit(h, y + 3)) % 2, r, far_set, 0, 1))
        return 4 * (y_ % 4) + 2 * (h_ % 2), set_

    def deliver(tile, number, wait=False):
        left, right = slots(tile)
        row, left_set = places(left)
        column, right_set = places(right)
        row, column = row + row_block, column + c
        mirror = number == 1
        dp_ = jnp.where(mirror, column, row)
        z_ = jnp.where(mirror, row, column)
        r_ = jnp.where(mirror, left_set, right_set)
        half = jnp.where(mirror, right_set, left_set)
        copy = remote(final.at[tile], staging.at[half, strip], final_send.at[tile, number], final_recv, (dp_, z_, r_))
        here = jnp.logical_and(jnp.logical_and(dp_ == dp, z_ == z), r_ == r)
        stay = pltpu.make_async_copy(final.at[tile], staging.at[half, strip], final_recv)

        @pl.when(jnp.logical_not(here))
        def _():
            if wait:
                copy.wait_send()
            else:
                copy.start()

        if not wait:

            @pl.when(here)
            def _():
                stay.start()

    def deliver_tile(tile, wait=False):
        @pl.loop(0, jnp.where(tile < 2, 1, 2))
        def _(number):
            deliver(tile, jnp.where(tile == 1, r, number), wait)

    def finish_tile(tile):
        sum_codes(tile)
        deliver_tile(tile)

    def finish_batch(batch):
        wait_codes(batch)
        over_tiles(batch, finish_tile)

    code_sends = [code_copies(batch) for batch in range(4)]

    def start_codes(batch):
        over_tiles(batch, encode_tile)
        for copy in code_sends[batch]:
            copy.start()

    for half in range(2):
        own_copies[half].wait()
        own_sends[half].wait_recv()
    over_tiles(0, product)

    for step in range(1, 16):
        source = (z + step) % 16
        remote(
            squares.at[source], squares.at[source], square_send.at[step], square_recv.at[source],
            device(y, h, c, z + step, r),
        ).wait_recv()
    inverse = lax.rsqrt(jnp.sum(squares[...], axis=0) + 1e-06)
    norm[0] = inverse[:, 0:128]
    norm[1] = inverse[:, 128:256]
    norm_sends = []
    for slot, half, y_, h_, r_ in wants:
        for core in range(2):
            norm_sends.append(
                remote(
                    norm.at[half], near_norm.at[slot, c], norm_send.at[slot, core], norm_recv.at[slot, c],
                    device(y_, h_, core, z, r_),
                )
            )
    for half in range(2):
        near_norm[OWN0 + half, c] = norm[half]
        norm_sends.append(
            remote(
                norm.at[half], near_norm.at[OWN0 + half, c], norm_send.at[4, half], norm_recv.at[4, half],
                device(y, h, 1 - c, z, r),
            )
        )
    for copy in norm_sends:
        copy.start()

    for half in range(2):
        remote(
            near_norm.at[OWN0 + half, 1 - c], near_norm.at[OWN0 + half, 1 - c], norm_send.at[4, half], norm_recv.at[4, half],
            device(y, h, 1 - c, z, r),
        ).wait_recv()
    for slot in (OWN0, OWN1):
        spread_norms(slot)
    over_tiles(0, join_cores)

    start_codes(0)

    def norm_arrived(slot):
        for core in range(2):
            remote(
                near_norm.at[slot, core], near_norm.at[slot, core],
                norm_send.at[slot, core], norm_recv.at[slot, core], device(y, h, 1 - c, z, r),
            ).wait_recv()

    def arrived(slot):
        for core in range(2):
            remote(
                near.at[slot, pl.ds(core * 128, 128)], near.at[slot, pl.ds(core * 128, 128)],
                gather_send.at[slot, core], gather_recv.at[slot, core], device(y, h, 1 - c, z, r),
            ).wait_recv()

    for slot in (UP, DOWN, OUT):
        norm_arrived(slot)
    for slot in (UP, DOWN):
        spread_norms(slot)

    for slot in (OUT, UP, DOWN):
        arrived(slot)
    far_copies = []
    for number, (slot, target) in enumerate(
        ((OUT, device(y + 2, h, c, z, r)), (UP, device(y + 3, h + 1, c, z, 1 - r)))
    ):
        rows = pl.ds(128 * number, 128)
        far_copies.append(
            remote(near.at[slot, rows], near.at[FAR, rows], far_sem.at[0, number], far_sem.at[1, number], target)
        )
        far_copies.append(
            remote(
                near_norm.at[slot, number], near_norm.at[FAR, number],
                far_sem.at[2, number], far_sem.at[3, number], target,
            )
        )

    @pl.when(even_chip)
    def _():
        for copy in far_copies:
            copy.start()

    over_tiles(1, product)
    over_tiles(2, product)
    over_tiles(1, join_cores)
    over_tiles(2, join_cores)
    start_codes(1)
    start_codes(2)
    finish_batch(0)

    @pl.when(even_chip)
    def _():
        for copy in far_copies:
            copy.wait_recv()

    over_tiles(3, product)
    over_tiles(3, join_cores)
    start_codes(3)
    finish_batch(1)
    finish_batch(2)
    finish_batch(3)

    pltpu.make_async_copy(staging, staging, final_recv).wait()
    for half in range(2):
        direct = is_direct(dp, z, r, half)

        @pl.when(direct)
        def _():
            out_ref[pl.ds(half * 128, 128), :] = decode(staging[half])

        @pl.when(jnp.logical_not(direct))
        def _():
            out_ref[pl.ds(half * 128, 128), :] = decode(staging[half]).T

    waits = gather + square_sends + own_sends + norm_sends
    for batch in range(4):
        waits += code_sends[batch]
    for copy in waits:
        copy.wait_send()

    @pl.when(even_chip)
    def _():
        for copy in far_copies:
            copy.wait_send()

    @pl.loop(0, TILE_COUNT)
    def _(tile):
        core_copy(tile).wait_send()
        for side in range(2):
            pair_copy(side, tile).wait_send()
        deliver_tile(tile, wait=True)


def body(grads):
    dma = pltpu.SemaphoreType.DMA
    return pl.pallas_call(
        kernel,
        out_shape=jax.ShapeDtypeStruct((256, 128), F32),
        in_specs=[pl.BlockSpec(memory_space=pltpu.HBM)],
        out_specs=pl.BlockSpec(memory_space=pltpu.VMEM),
        scratch_shapes=[
            pltpu.VMEM((256, FEATURES), BF16),
            pltpu.VMEM((6, 256, HALF), BF16),
            pltpu.VMEM((TILE_COUNT, 2, 256, 128), F32),
            pltpu.VMEM((TILE_COUNT, 256, 128), F32),
            pltpu.VMEM((TILE_COUNT, 4, 64, 128), F32),
            pltpu.VMEM((2, TILE_COUNT, 64, 128), BF16),
            pltpu.VMEM((2, TILE_COUNT, 64, 128), BF16),
            pltpu.VMEM((8, TILE_COUNT, 16, 128), BF16),
            pltpu.VMEM((8, TILE_COUNT, 16, 128), BF16),
            pltpu.VMEM((TILE_COUNT, 16, 128), BF16),
            pltpu.VMEM((2, 128, 128), BF16),
            pltpu.VMEM((16, 1, 256), F32),
            pltpu.VMEM((2, 1, 128), F32),
            pltpu.VMEM((6, 2, 1, 128), F32),
            pltpu.VMEM((6, 256, 128), F32),
            dma((3, 2)),
            dma((3, 2)),
            dma((2,)),
            dma((2,)),
            dma((2,)),
            dma((4, 2)),
            dma((16,)),
            dma((16,)),
            dma((5, 2)),
            dma((5, 2)),
            dma((TILE_COUNT,)),
            dma((TILE_COUNT,)),
            dma((TILE_COUNT, 2)),
            dma((TILE_COUNT, 2)),
            dma((4, 8)),
            dma((4, 8)),
            dma((TILE_COUNT, 2)),
            dma,
            dma,
        ],
        compiler_params=pltpu.CompilerParams(
            collective_id=0, has_side_effects=True, vmem_limit_bytes=60 * 1024 * 1024
        ),
        cost_estimate=pl.CostEstimate(flops=1510000000, bytes_accessed=1500000, transcendentals=0),
    )(grads)


def solution(mesh):
    in_specs = (P("dp", "layer"),)
    out_specs = P("dp", ("layer", "rep"))
    return jax.shard_map(body, mesh=mesh, in_specs=in_specs, out_specs=out_specs, check_vma=False)
```

time: 77.9 us -> 70.9 us (0.910)
  the two profiles are of different devices: /device:TPU:22 before, /device:TPU:54 now
where the time goes in v3:
time: 70.9 us; the launch traced here: 70.7 us
  Pallas kernels  69.1 us (97%)
  local copies, waits for them, and re-layouts  1.57 us (2%)
    pallas_call x1, Pallas kernels, body(): pl.pallas_call(kernel, out_shape=jax.ShapeDtypeStruct((256, 128), F32), i...  69.1 us
    unnamed x1, local copies, waits for them, and re-layouts  1.57 us

profile of v3, /device:TPU:54, one launch (start us, length us, event | category | flops | bytes accessed | tf_op | source)
XLA Modules:
  0.0 70.7 jit_solution(11043901555738801861)
XLA Ops:
  0.0 69.1 %shard_map.17 = f32[256,128]{1,0:T(8,128)} custom-call(bf16[256,2560]{1,0:T(8,128)(2,1)} %grads_ref.1), custom_call_target="tpu_custom_call" | custom-call | flops 1510000000 | bytes 1500000 | tf_op jit(solution)/shard_map/pallas_call | solution.py:449
  69.2 1.6 %copy.3 = f32[256,128]{1,0:T(8,128)} copy(f32[256,128]{1,0:T(8,128)} %shard_map.17) | data formatting | bytes 262144

commit v4 on v3

--- a/solution.py
+++ b/solution.py
@@ -79,8 +79,9 @@
     y, h, c = dp // 4, (dp // 2) % 2, dp % 2
     parity = (h + y) % 2
     g = (r + parity) % 2
-    odd = z % 2
+    quarter = z % 4
     even_chip = parity == 0
+    odd_chip = parity == 1
     last_slot = OUT + 1 - parity
 
     def device(y_, h_, c_, z_, r_):
@@ -192,12 +193,19 @@
         part[tile, 1] = value[:, 128:256]
         core_copy(tile).start()
 
-    pair_targets = (device(y, h, c, z + 1 - 2 * odd, r), device(y, h, c, z - 1 + 2 * odd, r))
-
-    def pair_copy(side, tile):
+    lanes = (
+        (device(y, h, c, z - 1, r), 0, 0, 64),
+        (device(y, h, c, z + 1, r), 1, 0, 64),
+        (device(y, h, c, z + 2, r), 2, 0, 32),
+        (device(y, h, c, z - 2, r), 2, 32, 32),
+    )
+
+    def near_copy(lane, tile):
+        target, place_, start, size = lanes[lane]
+        rows = pl.ds(start, size)
         return remote(
-            pair_code.at[side, tile], paired.at[side, tile], pair_send.at[tile, side], pair_recv.at[tile, side],
-            pair_targets[side],
+            pair_code.at[place_, tile, rows], paired.at[place_, tile, rows],
+            pair_send.at[tile, lane], pair_recv.at[tile, lane], target,
         )
 
     def join_cores(tile):
@@ -205,100 +213,108 @@
         core_copy(tile).wait_recv()
         value = (part[tile, c] + other[tile]) * row_scale[left] * near_norm[right, c]
         total[tile] = value.reshape(4, 64, 128)
-        for side in range(2):
-            pair_code[side, tile] = encode(total[tile, 2 * side + 1 - odd])
-            pair_copy(side, tile).start()
+        for index, step in enumerate((3, 1, 2)):
+            pair_code[index, tile] = encode(total[tile, (quarter + step) % 4])
+        for lane in range(4):
+            near_copy(lane, tile).start()
 
     def spread_norms(slot):
         for half in range(2):
             row_scale[slot, pl.ds(128 * half, 128)] = jnp.broadcast_to(near_norm[slot, half], (128, 128)).T
 
     def encode_tile(tile):
-        for side in range(2):
-            pair_copy(side, tile).wait_recv()
-            coded = encode(total[tile, 2 * side + odd] + decode(paired[side, tile]))
-            for j in range(4):
-                code[2 * j + side, tile] = coded[16 * j : 16 * j + 16]
+        for lane in range(4):
+            near_copy(lane, tile).wait_recv()
+        value = total[tile, quarter] + jnp.sum(decode(paired[:, tile]), axis=0)
+        coded = encode(value)
+        for j in range(4):
+            code[j, tile] = coded[16 * j : 16 * j + 16]
+        codes[z // 4, tile] = code[z // 4, tile]
 
     def code_copies(batch):
         first, count = BATCHES[batch]
         copies = []
-        for step in range(1, 8):
-            slot = (z // 2 + step) % 8
+        for step in range(1, 4):
+            slot = (z // 4 + step) % 4
             copies.append(
                 remote(
-                    code.at[slot, pl.ds(first, count)], codes.at[z // 2, pl.ds(first, count)],
-                    code_send.at[batch, step], code_recv.at[batch, z // 2],
-                    device(y, h, c, 2 * slot + odd, r),
+                    code.at[slot, pl.ds(first, count)], codes.at[z // 4, pl.ds(first, count)],
+                    code_send.at[batch, step], code_recv.at[batch, z // 4],
+                    device(y, h, c, 4 * slot + quarter, r),
                 )
             )
         return copies
 
     def wait_codes(batch):
         first, count = BATCHES[batch]
-        for step in range(1, 8):
-            slot = (z // 2 + step) % 8
+        for step in range(1, 4):
+            slot = (z // 4 + step) % 4
             remote(
                 codes.at[slot, pl.ds(first, count)], codes.at[slot, pl.ds(first, count)],
                 code_send.at[batch, step], code_recv.at[batch, slot],
-                device(y, h, c, 2 * slot + odd, r),
+                device(y, h, c, 4 * slot + quarter, r),
             ).wait_recv()
 
     def sum_codes(tile):
-        def add(step, value):
-            return value + decode(codes[(z // 2 + step) % 8, tile])
-
-        final[tile] = encode(lax.fori_loop(1, 8, add, decode(code[z // 2, tile])))
+        final[tile] = encode(jnp.sum(decode(codes[:, tile]), axis=0))
 
     row_block = (z % 4) // 2
     offset = pl.multiple_of(64 * (z % 2) + 16 * (z // 4), 16)
     strip = pl.ds(offset, 16)
-    def places(slot):
-        y_ = choose(slot, (y + 1, y + 3, y, y + 2, y, y))
-        h_ = choose(slot, (h, h, h + 1, h + 1, h, h))
-        far_set = jnp.where(c == 1, (1 - r + edge_bit(h + 1, y + 1)) % 2, r)
-        set_ = choose(slot, ((r + edge_bit(h, y)) % 2, (r + edge_bit(h, y + 3)) % 2, r, far_set, 0, 1))
-        return 4 * (y_ % 4) + 2 * (h_ % 2), set_
-
-    def deliver(tile, number, wait=False):
-        left, right = slots(tile)
-        row, left_set = places(left)
-        column, right_set = places(right)
+    far_set = jnp.where(c == 1, (1 - r + edge_bit(h + 1, y + 1 + h)) % 2, r)
+    home = 4 * y + 2 * h
+    across = 2 - 2 * h
+    places = {
+        UP: (4 * ((y + 1) % 4) + 2 * h, (r + edge_bit(h, y)) % 2),
+        DOWN: (4 * ((y + 3) % 4) + 2 * h, (r + edge_bit(h, y + 3)) % 2),
+        OUT: (4 * y + across, r),
+        OWN0: (home, 0),
+        OWN1: (home, 1),
+        "own": (home, g),
+        "last": (4 * ((y + 2 - 2 * parity) % 4) + across, jnp.where(even_chip, far_set, r)),
+    }
+    pairs = (
+        ("own", "own"), (OWN0, OWN1), ("own", UP), ("own", DOWN), (UP, DOWN), (UP, OUT), (DOWN, OUT),
+        (OWN0, "last"), (OWN1, "last"),
+    )
+    strips = []
+    for tile, (left, right) in enumerate(pairs):
+        row, left_set = places[left]
+        column, right_set = places[right]
         row, column = row + row_block, column + c
-        mirror = number == 1
-        dp_ = jnp.where(mirror, column, row)
-        z_ = jnp.where(mirror, row, column)
-        r_ = jnp.where(mirror, left_set, right_set)
-        half = jnp.where(mirror, right_set, left_set)
-        copy = remote(final.at[tile], staging.at[half, strip], final_send.at[tile, number], final_recv, (dp_, z_, r_))
-        here = jnp.logical_and(jnp.logical_and(dp_ == dp, z_ == z), r_ == r)
-        stay = pltpu.make_async_copy(final.at[tile], staging.at[half, strip], final_recv)
-
-        @pl.when(jnp.logical_not(here))
-        def _():
-            if wait:
-                copy.wait_send()
+        owner = (row, column, right_set, left_set)
+        mirror = (column, row, left_set, right_set)
+        if tile == 0:
+            targets = (owner,)
+        elif tile == 1:
+            targets = (tuple(jnp.where(r == 0, a, b) for a, b in zip(owner, mirror)),)
+        else:
+            targets = (owner, mirror)
+        for number, (dp_, z_, r_, half) in enumerate(targets):
+            copy = remote(
+                final.at[tile], staging.at[half, strip], final_send.at[tile, number], final_recv, (dp_, z_, r_)
+            )
+            here = None
+            if tile < 2 or (number == 0 and left in ("own", OWN0, OWN1)):
+                here = jnp.logical_and(jnp.logical_and(dp_ == dp, z_ == z), r_ == r)
+            strips.append((tile, copy, here, half))
+
+    def deliver(tile):
+        for tile_, copy, here, half in strips:
+            if tile_ != tile:
+                continue
+            if here is None:
+                copy.start()
             else:
-                copy.start()
-
-        if not wait:
-
-            @pl.when(here)
-            def _():
-                stay.start()
-
-    def deliver_tile(tile, wait=False):
-        @pl.loop(0, jnp.where(tile < 2, 1, 2))
-        def _(number):
-            deliver(tile, jnp.where(tile == 1, r, number), wait)
-
-    def finish_tile(tile):
-        sum_codes(tile)
-        deliver_tile(tile)
+                pl.when(jnp.logical_not(here))(copy.start)
+                pl.when(here)(pltpu.make_async_copy(final.at[tile], staging.at[half, strip], final_recv).start)
 
     def finish_batch(batch):
         wait_codes(batch)
-        over_tiles(batch, finish_tile)
+        first, count = BATCHES[batch]
+        for tile in range(first, first + count):
+            sum_codes(tile)
+            deliver(tile)
 
     code_sends = [code_copies(batch) for batch in range(4)]
 
@@ -375,7 +391,7 @@
         arrived(slot)
     far_copies = []
     for number, (slot, target) in enumerate(
-        ((OUT, device(y + 2, h, c, z, r)), (UP, device(y + 3, h + 1, c, z, 1 - r)))
+        ((OUT, device(y + 2, h, c, z, r)), (DOWN - h, device(y + 1 + 2 * h, h + 1, c, z, 1 - r)))
     ):
         rows = pl.ds(128 * number, 128)
         far_copies.append(
@@ -395,35 +411,38 @@
 
     over_tiles(1, product)
     over_tiles(2, product)
+
+    @pl.when(odd_chip)
+    def _():
+        over_tiles(3, product)
+
     over_tiles(1, join_cores)
     over_tiles(2, join_cores)
+
+    @pl.when(odd_chip)
+    def _():
+        over_tiles(3, join_cores)
+
     start_codes(1)
     start_codes(2)
+
+    @pl.when(odd_chip)
+    def _():
+        start_codes(3)
+
     finish_batch(0)
 
     @pl.when(even_chip)
     def _():
         for copy in far_copies:
             copy.wait_recv()
-
-    over_tiles(3, product)
-    over_tiles(3, join_cores)
-    start_codes(3)
+        over_tiles(3, product)
+        over_tiles(3, join_cores)
+        start_codes(3)
+
     finish_batch(1)
     finish_batch(2)
     finish_batch(3)
-
-    pltpu.make_async_copy(staging, staging, final_recv).wait()
-    for half in range(2):
-        direct = is_direct(dp, z, r, half)
-
-        @pl.when(direct)
-        def _():
-            out_ref[pl.ds(half * 128, 128), :] = decode(staging[half])
-
-        @pl.when(jnp.logical_not(direct))
-        def _():
-            out_ref[pl.ds(half * 128, 128), :] = decode(staging[half]).T
 
     waits = gather + square_sends + own_sends + norm_sends
     for batch in range(4):
@@ -439,9 +458,26 @@
     @pl.loop(0, TILE_COUNT)
     def _(tile):
         core_copy(tile).wait_send()
-        for side in range(2):
-            pair_copy(side, tile).wait_send()
-        deliver_tile(tile, wait=True)
+        for lane in range(4):
+            near_copy(lane, tile).wait_send()
+
+    for _, copy, here, _ in strips:
+        if here is None:
+            copy.wait_send()
+        else:
+            pl.when(jnp.logical_not(here))(copy.wait_send)
+
+    pltpu.make_async_copy(staging, staging, final_recv).wait()
+    for half in range(2):
+        direct = is_direct(dp, z, r, half)
+
+        @pl.when(direct)
+        def _():
+            out_ref[pl.ds(half * 128, 128), :] = decode(staging[half])
+
+        @pl.when(jnp.logical_not(direct))
+        def _():
+            out_ref[pl.ds(half * 128, 128), :] = decode(staging[half]).T
 
 
 def body(grads):
@@ -457,10 +493,10 @@
             pltpu.VMEM((TILE_COUNT, 2, 256, 128), F32),
             pltpu.VMEM((TILE_COUNT, 256, 128), F32),
             pltpu.VMEM((TILE_COUNT, 4, 64, 128), F32),
-            pltpu.VMEM((2, TILE_COUNT, 64, 128), BF16),
-            pltpu.VMEM((2, TILE_COUNT, 64, 128), BF16),
-            pltpu.VMEM((8, TILE_COUNT, 16, 128), BF16),
-            pltpu.VMEM((8, TILE_COUNT, 16, 128), BF16),
+            pltpu.VMEM((3, TILE_COUNT, 64, 128), BF16),
+            pltpu.VMEM((3, TILE_COUNT, 64, 128), BF16),
+            pltpu.VMEM((4, TILE_COUNT, 16, 128), BF16),
+            pltpu.VMEM((4, TILE_COUNT, 16, 128), BF16),
             pltpu.VMEM((TILE_COUNT, 16, 128), BF16),
             pltpu.VMEM((2, 128, 128), BF16),
             pltpu.VMEM((16, 1, 256), F32),
@@ -479,10 +515,10 @@
             dma((5, 2)),
             dma((TILE_COUNT,)),
             dma((TILE_COUNT,)),
-            dma((TILE_COUNT, 2)),
-            dma((TILE_COUNT, 2)),
-            dma((4, 8)),
-            dma((4, 8)),
+            dma((TILE_COUNT, 4)),
+            dma((TILE_COUNT, 4)),
+            dma((4, 4)),
+            dma((4, 4)),
             dma((TILE_COUNT, 2)),
             dma,
             dma,

time: 70.9 us -> 68.4 us (0.965)
  the two profiles are of different devices: /device:TPU:54 before, /device:TPU:22 now
where the time goes in v4:
time: 68.4 us; the launch traced here: 68.3 us
  Pallas kernels  66.7 us (98%)
  local copies, waits for them, and re-layouts  1.57 us (2%)
    pallas_call x1, Pallas kernels, body(): pl.pallas_call(kernel, out_shape=jax.ShapeDtypeStruct((256, 128), F32), i...  66.7 us
    unnamed x1, local copies, waits for them, and re-layouts  1.57 us

profile of v4, /device:TPU:22, one launch (start us, length us, event | category | flops | bytes accessed | tf_op | source)
XLA Modules:
  0.0 68.3 jit_solution(16704050094841027553)
XLA Ops:
  0.0 66.7 %shard_map.17 = f32[256,128]{1,0:T(8,128)} custom-call(bf16[256,2560]{1,0:T(8,128)(2,1)} %grads_ref.1), custom_call_target="tpu_custom_call" | custom-call | flops 1510000000 | bytes 1500000 | tf_op jit(solution)/shard_map/pallas_call | solution.py:485
  66.7 1.6 %copy.3 = f32[256,128]{1,0:T(8,128)} copy(f32[256,128]{1,0:T(8,128)} %shard_map.17) | data formatting | bytes 262144

commit v5 on v4

--- a/solution.py
+++ b/solution.py
@@ -15,8 +15,8 @@
 CODE_SHIFT = 2.0**-7.5
 CODE_SCALE = 13.4
 UP, DOWN, OUT, FAR, OWN0, OWN1 = range(6)
-TILE_COUNT = 9
-BATCHES = ((0, 2), (2, 2), (4, 3), (7, 2))
+TILE_COUNT = 11
+BATCHES = ((0, 2), (2, 4), (6, 3), (9, 2))
 
 
 def edge_bit(h, y):
@@ -27,7 +27,7 @@
     yd, hd = dp // 4, (dp // 2) % 2
     yl, hl = layer // 4, (layer // 2) % 2
     dh, dy = (hl + hd) % 2, (yl - yd + 4) % 4
-    parity = (hd + yd) % 2
+    parity = (hd + yd + 1) % 2
     mixed = (half + rep) % 2
     above = edge_bit(hd, yd)
     second = edge_bit(hd, yd + 1)
@@ -35,11 +35,7 @@
     same_column = jnp.where(
         dy == 0,
         jnp.where(mixed == 0, 0, half),
-        jnp.where(
-            dy == 1,
-            (mixed + parity + above) % 2,
-            jnp.where(dy == 3, (mixed + parity + below) % 2, (mixed + above + second + 1) % 2),
-        ),
+        jnp.where(dy == 2, (mixed + above + second + 1) % 2, 1 - parity),
     )
     other_column = jnp.where(
         dy == 1,
@@ -71,13 +67,13 @@
     squares, norm, near_norm, row_scale,
     gather_send, gather_recv, own_send, own_recv, local_sem, far_sem, square_send, square_recv,
     norm_send, norm_recv, core_send, core_recv, pair_send, pair_recv, code_send, code_recv,
-    final_send, final_recv, load_sem,
+    final_send, final_recv, load_sem, entered,
 ):
     dp = lax.axis_index("dp")
     z = lax.axis_index("layer")
     r = lax.axis_index("rep")
     y, h, c = dp // 4, (dp // 2) % 2, dp % 2
-    parity = (h + y) % 2
+    parity = (h + y + 1) % 2
     g = (r + parity) % 2
     quarter = z % 4
     even_chip = parity == 0
@@ -100,53 +96,33 @@
     partners += [device(y + 1, h + 1, c, z, 1 - r), device(y + 3, h + 1, c, z, 1 - r)]
     for core in range(2):
         partners += [device(y + 1, h, core, z, r), device(y + 3, h, core, z, r), device(y, h + 1, core, z, 1 - r)]
+    partners += [device(y, h, c, z + step, r) for step in (-3, -2, -1, 1, 2, 3)]
     for target in partners:
         pl.semaphore_signal(barrier, inc=1, device_id=target, device_id_type=MESH)
-    for step in range(1, 16):
-        pl.semaphore_signal(barrier, inc=1, device_id=device(y, h, c, z + step, r), device_id_type=MESH)
-
     load.wait()
-
-    @pl.loop(0, 8)
-    def _(group):
-        wide = g_ref[pl.ds(pl.multiple_of(group * 32, 32), 32), :].astype(F32)
-        local = jnp.sum(wide * wide, axis=1, keepdims=True)
-        row_scale[0, pl.ds(pl.multiple_of(group * 32, 32), 32)] = jnp.broadcast_to(local, (32, 128))
-
-    squares[z] = row_scale[0].T[0:1, :]
-
-    pl.semaphore_wait(barrier, len(partners) + 15)
+    pl.semaphore_wait(barrier, len(partners))
 
     wants = (
         (UP, (r + edge_bit(h, y + 3)) % 2, y + 3, h, r),
         (DOWN, (r + edge_bit(h, y)) % 2, y + 1, h, r),
         (OUT, 1 - r, y, h + 1, 1 - r),
     )
-    def gather_copies(slot, half, y_, h_, r_):
-        rows = pl.ds(pl.multiple_of(half * 128, 128), 128)
+    def gather_copies(part_, slot, half, y_, h_, r_):
+        rows = pl.ds(pl.multiple_of(half * 128 + part_ * 64, 64), 64)
         return [
             remote(
                 g_ref.at[rows, pl.ds(core * HALF, HALF)],
-                near.at[slot, pl.ds(pl.multiple_of(c * 128, 128), 128)],
-                gather_send.at[slot, core],
-                gather_recv.at[slot, c],
+                near.at[slot, pl.ds(pl.multiple_of(c * 128 + part_ * 64, 64), 64)],
+                gather_send.at[slot, core, part_],
+                gather_recv.at[slot, c, part_],
                 device(y_, h_, core, z, r_),
             )
             for core in range(2)
         ]
 
-    gather = [copy for want in wants for copy in gather_copies(*want)]
+    gather = [copy for part_ in range(2) for want in wants for copy in gather_copies(part_, *want)]
     for copy in gather:
         copy.start()
-    square_sends = []
-    for step in range(1, 16):
-        square_sends.append(
-            remote(
-                squares.at[z], squares.at[z], square_send.at[step], square_recv.at[z],
-                device(y, h, c, z + step, r),
-            )
-        )
-        square_sends[-1].start()
     mine = pl.ds(pl.multiple_of(c * HALF, 128), HALF)
     theirs = pl.ds(pl.multiple_of((1 - c) * HALF, 128), HALF)
     place = pl.ds(pl.multiple_of(c * 128, 128), 128)
@@ -164,6 +140,28 @@
     for copy in own_sends + own_copies:
         copy.start()
 
+    @pl.loop(0, 8)
+    def _(group):
+        wide = g_ref[pl.ds(pl.multiple_of(group * 32, 32), 32), :].astype(F32)
+        local = jnp.sum(wide * wide, axis=1, keepdims=True)
+        row_scale[0, pl.ds(pl.multiple_of(group * 32, 32), 32)] = jnp.broadcast_to(local, (32, 128))
+
+    squares[z] = row_scale[0].T[0:1, :]
+    for stage in range(2):
+        for step in (-3, 3):
+            pl.semaphore_signal(
+                entered.at[stage], inc=1, device_id=device(y, h, c, z + step, r), device_id_type=MESH
+            )
+        pl.semaphore_wait(entered.at[stage], 2)
+    square_sends = []
+    for step in range(1, 16):
+        square_sends.append(
+            remote(
+                squares.at[z], squares.at[z], square_send.at[step], square_recv.at[z],
+                device(y, h, c, z + step, r),
+            )
+        )
+        square_sends[-1].start()
     def choose(tile, values):
         chosen = values[-1]
         for index in range(len(values) - 2, -1, -1):
@@ -173,8 +171,8 @@
     own = OWN0 + g
 
     def slots(tile):
-        left = choose(tile, (own, OWN0, own, own, UP, UP, DOWN, OWN0, OWN1))
-        right = choose(tile, (own, OWN1, UP, DOWN, DOWN, OUT, OUT, last_slot, last_slot))
+        left = choose(tile, (own, OWN0, OWN0, OWN1, OWN0, OWN1, UP, UP, DOWN, OWN0, OWN1))
+        right = choose(tile, (own, OWN1, UP, UP, DOWN, DOWN, DOWN, OUT, OUT, last_slot, last_slot))
         return left, right
 
     def core_copy(tile):
@@ -261,7 +259,7 @@
     row_block = (z % 4) // 2
     offset = pl.multiple_of(64 * (z % 2) + 16 * (z // 4), 16)
     strip = pl.ds(offset, 16)
-    far_set = jnp.where(c == 1, (1 - r + edge_bit(h + 1, y + 1 + h)) % 2, r)
+    far_set = jnp.where(c == 1, (1 - r + edge_bit(h + 1, y + 1 + y % 2)) % 2, r)
     home = 4 * y + 2 * h
     across = 2 - 2 * h
     places = {
@@ -274,8 +272,8 @@
         "last": (4 * ((y + 2 - 2 * parity) % 4) + across, jnp.where(even_chip, far_set, r)),
     }
     pairs = (
-        ("own", "own"), (OWN0, OWN1), ("own", UP), ("own", DOWN), (UP, DOWN), (UP, OUT), (DOWN, OUT),
-        (OWN0, "last"), (OWN1, "last"),
+        ("own", "own"), (OWN0, OWN1), (OWN0, UP), (OWN1, UP), (OWN0, DOWN), (OWN1, DOWN),
+        (UP, DOWN), (UP, OUT), (DOWN, OUT), (OWN0, "last"), (OWN1, "last"),
     )
     strips = []
     for tile, (left, right) in enumerate(pairs):
@@ -366,8 +364,6 @@
         spread_norms(slot)
     over_tiles(0, join_cores)
 
-    start_codes(0)
-
     def norm_arrived(slot):
         for core in range(2):
             remote(
@@ -375,97 +371,127 @@
                 norm_send.at[slot, core], norm_recv.at[slot, core], device(y, h, 1 - c, z, r),
             ).wait_recv()
 
-    def arrived(slot):
-        for core in range(2):
-            remote(
-                near.at[slot, pl.ds(core * 128, 128)], near.at[slot, pl.ds(core * 128, 128)],
-                gather_send.at[slot, core], gather_recv.at[slot, core], device(y, h, 1 - c, z, r),
-            ).wait_recv()
+    def arrived(slot, core, part_):
+        rows = pl.ds(core * 128 + part_ * 64, 64)
+        remote(
+            near.at[slot, rows], near.at[slot, rows],
+            gather_send.at[slot, core, part_], gather_recv.at[slot, core, part_], device(y, h, 1 - c, z, r),
+        ).wait_recv()
 
     for slot in (UP, DOWN, OUT):
         norm_arrived(slot)
     for slot in (UP, DOWN):
         spread_norms(slot)
 
-    for slot in (OUT, UP, DOWN):
-        arrived(slot)
     far_copies = []
-    for number, (slot, target) in enumerate(
-        ((OUT, device(y + 2, h, c, z, r)), (DOWN - h, device(y + 1 + 2 * h, h + 1, c, z, 1 - r)))
-    ):
-        rows = pl.ds(128 * number, 128)
-        far_copies.append(
-            remote(near.at[slot, rows], near.at[FAR, rows], far_sem.at[0, number], far_sem.at[1, number], target)
-        )
-        far_copies.append(
-            remote(
-                near_norm.at[slot, number], near_norm.at[FAR, number],
-                far_sem.at[2, number], far_sem.at[3, number], target,
-            )
-        )
+
+    def forward(number, part_):
+        slot, target = (
+            (OUT, device(y + 2, h, c, z, r)), (DOWN - y % 2, device(y + 1 + 2 * (y % 2), h + 1, c, z, 1 - r))
+        )[number]
+        arrived(slot, number, part_)
+        rows = pl.ds(128 * number + 64 * part_, 64)
+        copies = [
+            remote(
+                near.at[slot, rows], near.at[FAR, rows],
+                far_sem.at[0, number, part_], far_sem.at[1, number, part_], target,
+            )
+        ]
+        if part_ == 0:
+            copies.append(
+                remote(
+                    near_norm.at[slot, number], near_norm.at[FAR, number],
+                    far_sem.at[2, number, 0], far_sem.at[2, number, 1], target,
+                )
+            )
+
+        @pl.when(even_chip)
+        def _():
+            for copy in copies:
+                copy.start()
+
+        far_copies.extend(copies)
+
+    forward(0, 0)
+    forward(1, 0)
+    start_codes(0)
+
+    forward(0, 1)
+    forward(1, 1)
+    for part_ in range(2):
+        arrived(OUT, 1, part_)
+        arrived(DOWN - y % 2, 0, part_)
+        for core in range(2):
+            arrived(UP + y % 2, core, part_)
+
+    @pl.when(odd_chip)
+    def _():
+        over_tiles(1, product)
+        over_tiles(2, product)
+        over_tiles(1, join_cores)
+        over_tiles(3, product)
+        over_tiles(2, join_cores)
+        over_tiles(3, join_cores)
+        start_codes(1)
+        start_codes(2)
+        start_codes(3)
+        finish_batch(0)
+        finish_batch(1)
+        finish_batch(2)
+        finish_batch(3)
 
     @pl.when(even_chip)
     def _():
-        for copy in far_copies:
-            copy.start()
-
-    over_tiles(1, product)
-    over_tiles(2, product)
-
-    @pl.when(odd_chip)
-    def _():
-        over_tiles(3, product)
-
-    over_tiles(1, join_cores)
-    over_tiles(2, join_cores)
-
-    @pl.when(odd_chip)
-    def _():
-        over_tiles(3, join_cores)
-
-    start_codes(1)
-    start_codes(2)
-
-    @pl.when(odd_chip)
-    def _():
-        start_codes(3)
-
-    finish_batch(0)
-
-    @pl.when(even_chip)
-    def _():
+        over_tiles(2, product)
+        over_tiles(2, join_cores)
+        start_codes(2)
+        finish_batch(0)
         for copy in far_copies:
             copy.wait_recv()
         over_tiles(3, product)
         over_tiles(3, join_cores)
+        finish_batch(2)
         start_codes(3)
-
-    finish_batch(1)
-    finish_batch(2)
-    finish_batch(3)
+        finish_batch(3)
 
     waits = gather + square_sends + own_sends + norm_sends
-    for batch in range(4):
+    for batch in (0, 2, 3):
         waits += code_sends[batch]
     for copy in waits:
         copy.wait_send()
+
+    def sent(tile):
+        core_copy(tile).wait_send()
+        for lane in range(4):
+            near_copy(lane, tile).wait_send()
+
+    def delivered(batch):
+        first, count = BATCHES[batch]
+        for tile, copy, here, _ in strips:
+            if not first <= tile < first + count:
+                continue
+            if here is None:
+                copy.wait_send()
+            else:
+                pl.when(jnp.logical_not(here))(copy.wait_send)
+
+    for batch in (0, 2, 3):
+        over_tiles(batch, sent)
+
+    @pl.when(odd_chip)
+    def _():
+        for copy in code_sends[1]:
+            copy.wait_send()
+        over_tiles(1, sent)
+        delivered(1)
 
     @pl.when(even_chip)
     def _():
         for copy in far_copies:
             copy.wait_send()
 
-    @pl.loop(0, TILE_COUNT)
-    def _(tile):
-        core_copy(tile).wait_send()
-        for lane in range(4):
-            near_copy(lane, tile).wait_send()
-
-    for _, copy, here, _ in strips:
-        if here is None:
-            copy.wait_send()
-        else:
-            pl.when(jnp.logical_not(here))(copy.wait_send)
+    for batch in (0, 2, 3):
+        delivered(batch)
 
     pltpu.make_async_copy(staging, staging, final_recv).wait()
     for half in range(2):
@@ -503,12 +529,12 @@
             pltpu.VMEM((2, 1, 128), F32),
             pltpu.VMEM((6, 2, 1, 128), F32),
             pltpu.VMEM((6, 256, 128), F32),
-            dma((3, 2)),
-            dma((3, 2)),
+            dma((3, 2, 2)),
+            dma((3, 2, 2)),
             dma((2,)),
             dma((2,)),
             dma((2,)),
-            dma((4, 2)),
+            dma((3, 2, 2)),
             dma((16,)),
             dma((16,)),
             dma((5, 2)),
@@ -522,6 +548,7 @@
             dma((TILE_COUNT, 2)),
             dma,
             dma,
+            pltpu.SemaphoreType.REGULAR((2,)),
         ],
         compiler_params=pltpu.CompilerParams(
             collective_id=0, has_side_effects=True, vmem_limit_bytes=60 * 1024 * 1024

time: 68.4 us -> 65.5 us (0.958)
  the two profiles are of different devices: /device:TPU:22 before, /device:TPU:6 now
where the time goes in v5:
time: 65.5 us; the launch traced here: 65.3 us
  Pallas kernels  63.8 us (97%)
  local copies, waits for them, and re-layouts  1.57 us (2%)
    pallas_call x1, Pallas kernels, body(): pl.pallas_call(kernel, out_shape=jax.ShapeDtypeStruct((256, 128), F32), i...  63.8 us
    unnamed x1, local copies, waits for them, and re-layouts  1.57 us

profile of v5, /device:TPU:6, one launch (start us, length us, event | category | flops | bytes accessed | tf_op | source)
XLA Modules:
  0.0 65.3 jit_solution(14168253935696979859)
XLA Ops:
  0.0 63.8 %shard_map.17 = f32[256,128]{1,0:T(8,128)} custom-call(bf16[256,2560]{1,0:T(8,128)(2,1)} %grads_ref.1), custom_call_target="tpu_custom_call" | custom-call | flops 1510000000 | bytes 1500000 | tf_op jit(solution)/shard_map/pallas_call | solution.py:511
  63.8 1.6 %copy.3 = f32[256,128]{1,0:T(8,128)} copy(f32[256,128]{1,0:T(8,128)} %shard_map.17) | data formatting | bytes 262144

commit v6 on v5

--- a/solution.py
+++ b/solution.py
@@ -96,7 +96,7 @@
     partners += [device(y + 1, h + 1, c, z, 1 - r), device(y + 3, h + 1, c, z, 1 - r)]
     for core in range(2):
         partners += [device(y + 1, h, core, z, r), device(y + 3, h, core, z, r), device(y, h + 1, core, z, 1 - r)]
-    partners += [device(y, h, c, z + step, r) for step in (-3, -2, -1, 1, 2, 3)]
+    partners += [device(y, h, c, z + step, r) for step in (-4, -3, -2, -1, 1, 2, 3, 4)]
     for target in partners:
         pl.semaphore_signal(barrier, inc=1, device_id=target, device_id_type=MESH)
     load.wait()
@@ -147,12 +147,9 @@
         row_scale[0, pl.ds(pl.multiple_of(group * 32, 32), 32)] = jnp.broadcast_to(local, (32, 128))
 
     squares[z] = row_scale[0].T[0:1, :]
-    for stage in range(2):
-        for step in (-3, 3):
-            pl.semaphore_signal(
-                entered.at[stage], inc=1, device_id=device(y, h, c, z + step, r), device_id_type=MESH
-            )
-        pl.semaphore_wait(entered.at[stage], 2)
+    for step in (-4, 4):
+        pl.semaphore_signal(entered, inc=1, device_id=device(y, h, c, z + step, r), device_id_type=MESH)
+    pl.semaphore_wait(entered, 2)
     square_sends = []
     for step in range(1, 16):
         square_sends.append(
@@ -297,9 +294,9 @@
                 here = jnp.logical_and(jnp.logical_and(dp_ == dp, z_ == z), r_ == r)
             strips.append((tile, copy, here, half))
 
-    def deliver(tile):
-        for tile_, copy, here, half in strips:
-            if tile_ != tile:
+    def deliver(first, count):
+        for tile, copy, here, half in sorted(strips, key=lambda entry: entry[2] is not None):
+            if not first <= tile < first + count:
                 continue
             if here is None:
                 copy.start()
@@ -312,7 +309,7 @@
         first, count = BATCHES[batch]
         for tile in range(first, first + count):
             sum_codes(tile)
-            deliver(tile)
+        deliver(first, count)
 
     code_sends = [code_copies(batch) for batch in range(4)]
 
@@ -412,12 +409,11 @@
 
         far_copies.extend(copies)
 
-    forward(0, 0)
-    forward(1, 0)
     start_codes(0)
 
-    forward(0, 1)
-    forward(1, 1)
+    for part_ in range(2):
+        forward(0, part_)
+        forward(1, part_)
     for part_ in range(2):
         arrived(OUT, 1, part_)
         arrived(DOWN - y % 2, 0, part_)
@@ -427,18 +423,18 @@
     @pl.when(odd_chip)
     def _():
         over_tiles(1, product)
+        over_tiles(3, product)
+        over_tiles(1, join_cores)
         over_tiles(2, product)
-        over_tiles(1, join_cores)
-        over_tiles(3, product)
+        over_tiles(3, join_cores)
         over_tiles(2, join_cores)
-        over_tiles(3, join_cores)
         start_codes(1)
+        start_codes(3)
         start_codes(2)
-        start_codes(3)
         finish_batch(0)
         finish_batch(1)
+        finish_batch(3)
         finish_batch(2)
-        finish_batch(3)
 
     @pl.when(even_chip)
     def _():
@@ -450,8 +446,8 @@
             copy.wait_recv()
         over_tiles(3, product)
         over_tiles(3, join_cores)
+        start_codes(3)
         finish_batch(2)
-        start_codes(3)
         finish_batch(3)
 
     waits = gather + square_sends + own_sends + norm_sends
@@ -548,7 +544,7 @@
             dma((TILE_COUNT, 2)),
             dma,
             dma,
-            pltpu.SemaphoreType.REGULAR((2,)),
+            pltpu.SemaphoreType.REGULAR,
         ],
         compiler_params=pltpu.CompilerParams(
             collective_id=0, has_side_effects=True, vmem_limit_bytes=60 * 1024 * 1024

time: 65.5 us -> 64.6 us (0.986)
  the two profiles are of different devices: /device:TPU:6 before, /device:TPU:112 now
where the time goes in v6:
time: 64.6 us; the launch traced here: 64.5 us
  Pallas kernels  62.9 us (97%)
  local copies, waits for them, and re-layouts  1.57 us (2%)
    pallas_call x1, Pallas kernels, body(): pl.pallas_call(kernel, out_shape=jax.ShapeDtypeStruct((256, 128), F32), i...  62.9 us
    unnamed x1, local copies, waits for them, and re-layouts  1.57 us

profile of v6, /device:TPU:112, one launch (start us, length us, event | category | flops | bytes accessed | tf_op | source)
XLA Modules:
  0.0 64.5 jit_solution(14883594139160888048)
XLA Ops:
  0.0 62.9 %shard_map.17 = f32[256,128]{1,0:T(8,128)} custom-call(bf16[256,2560]{1,0:T(8,128)(2,1)} %grads_ref.1), custom_call_target="tpu_custom_call" | custom-call | flops 1510000000 | bytes 1500000 | tf_op jit(solution)/shard_map/pallas_call | solution.py:507
  62.9 1.6 %copy.3 = f32[256,128]{1,0:T(8,128)} copy(f32[256,128]{1,0:T(8,128)} %shard_map.17) | data formatting | bytes 262144
